TPU v7x, 32 devices: a whole 2x2x4 slice. The times are simulated.
32 devices in a mesh: pair: 8 (over y, x, core), ph: 4 (over z).
Axes of the slice: x: 2, y: 2, z: 4, core: 2. Of those that a mesh axis runs over, the one named last changes fastest.
Arguments:
- t_cycle: float32 [8, 512, 8192], P(None, 'pair', 'ph'), may hold values from -6 to 6
- w_cycle: float32 [8, 8192, 4096], P(None, 'ph', 'pair'), may hold values from -0.1875 to 0.1875
- occ_energy: float32 [64], replicated, may hold values from -1.5 to -0.5
- vir_energy: float32 [8, 128], replicated, may hold values from 0.2 to 1.5
- occ_irrep: int32 [64], replicated, may hold values from 0 to 7
- vir_count: int32 [8], replicated, may hold values from 1 to 128, 640 in all
Outputs:
- increment: float32 [8, 512, 4096], P(None, 'ph', 'pair')
Inputs may be any that keep to these rules, and one draw needn't show every extreme that they name: `occ_irrep`: irrep labels combine by exclusive or. `vir_count`: the counts sum to 640; one irrep fills all 128 slots.
All inputs are finite; a program needn't handle non-finite values.
Results may differ from a plain program's by a relative error of at most 0.000075.
Values sent between devices are 32-bit elements; how exact they have to be, the bound alone decides.
A program may use at most 128 MiB of HBM per device.

v0:
```python
import jax
import jax.numpy as jnp
from jax import lax
from jax.sharding import PartitionSpec as P

IRREPS = 8
VIRT_CAP = 128
ROW_OCC = 4
COL_OCC = 32
ROWS = 512
PAIRS = 8192
COLS = 4096


def reduce_rows(partial_value):
    return lax.psum_scatter(partial_value, "ph", scatter_dimension=1, tiled=True)


def on_device(t_cycle, w_cycle, occ_energy, vir_energy, occ_irrep, vir_count):
    n_pair = lax.axis_size("pair")
    n_ph = lax.axis_size("ph")
    ph_index = lax.axis_index("ph")
    pair_index = lax.axis_index("pair")
    local_rows = t_cycle.shape[1]
    local_pairs = t_cycle.shape[2]
    local_cols = w_cycle.shape[2]
    out_rows = local_rows * n_pair // n_ph
    slot_ids = jnp.arange(VIRT_CAP, dtype=jnp.int32)
    irreps = jnp.arange(IRREPS, dtype=jnp.int32)
    symmetry = jnp.bitwise_xor(occ_irrep[None, :], irreps[:, None])
    onehot = symmetry[:, :, None] == irreps[None, None, :]
    counts = jnp.sum(jnp.where(onehot, vir_count[None, None, :], 0), axis=2)
    live_slot = (slot_ids[None, None, :] < counts[:, :, None]).astype(jnp.float32)
    vir_ener = jnp.einsum(
        "goh,hv->gov",
        onehot.astype(jnp.float32),
        vir_energy,
        precision=lax.Precision.HIGHEST,
        preferred_element_type=jnp.float32,
    )
    mask_pair = lax.dynamic_slice_in_dim(
        live_slot.reshape(IRREPS, PAIRS), ph_index * local_pairs, local_pairs, 1
    )
    w_masked = w_cycle * mask_pair[:, :, None]
    mask_row = lax.dynamic_slice_in_dim(
        live_slot[:, :ROW_OCC].reshape(IRREPS, ROWS), ph_index * out_rows, out_rows, 1
    )
    mask_col = lax.dynamic_slice_in_dim(
        live_slot[:, :COL_OCC].reshape(IRREPS, COLS), pair_index * local_cols, local_cols, 1
    )
    e_row = (occ_energy[None, :ROW_OCC, None] - vir_ener[:, :ROW_OCC]).reshape(IRREPS, ROWS)
    e_col = (occ_energy[None, :COL_OCC, None] - vir_ener[:, :COL_OCC]).reshape(IRREPS, COLS)
    e_row = lax.dynamic_slice_in_dim(e_row, ph_index * out_rows, out_rows, 1)
    e_col = lax.dynamic_slice_in_dim(e_col, pair_index * local_cols, local_cols, 1)
    partial_value = jnp.einsum(
        "grk,gkc->grc",
        lax.all_gather(t_cycle, "pair", axis=1, tiled=True),
        w_masked,
        precision=lax.Precision.HIGHEST,
        preferred_element_type=jnp.float32,
    )
    summed = reduce_rows(partial_value)
    return (
        mask_row[:, :, None]
        * mask_col[:, None, :]
        * summed
        / (e_row[:, :, None] + e_col[:, None, :])
    )


def solution(mesh):
    return jax.shard_map(
        on_device,
        mesh=mesh,
        in_specs=(P(None, "pair", "ph"), P(None, "ph", "pair"), P(), P(), P(), P()),
        out_specs=P(None, "ph", "pair"),
        check_vma=False,
    )
```

profile of v0, /device:TPU:0, one launch (start us, length us, event | category | flops | bytes accessed | tf_op | source)
XLA Modules:
  0.0 441.0 jit_solution(17272154096681084053)
XLA Ops:
  6.5 0.0 copy-start
  6.5 0.0 copy-start.2
  6.5 0.0 copy-start.3
  6.5 0.0 all-gather.2.cloned.1.call-start
  6.5 0.7 all-gather.2.cloned.1.call-update
  7.3 0.0 reduce-scatter.2.cloned.1.call-start
  7.3 0.0 copy-done.2
  7.3 0.0 copy-done.3
  7.3 0.1 select_reduce_fusion
  7.4 0.1 copy.9
  7.5 0.1 broadcast_bitcast_fusion
  7.7 165.1 %all-gather.2.cloned.1.call-done = f32[8,512,2048]{2,1,0:T(8,128)} async-done(((f32[8,64,2048]{2,1,0:T(8,128)}), f32[8,512,2048]{2,1,0:T(8,128)}) %all-gather.2.cloned.1.call-update) | async-done | bytes 33554448 | tf_op jit(solution)/shard_map/all_gather | solution.py:57
  172.8 112.4 %fusion.3 = f32[8,512,512]{1,2,0:T(8,128)} fusion(f32[8,512,2048]{2,1,0:T(8,128)} %all-gather.2.cloned.1.call-done, f32[8,2048,512]{2,1,0:T(8,128)} %param.7, f32[8,2048]{1,0:T(8,128)S(1)} %fusion.8), kind=kOutput, calls=%fused_computation.3 | convolution fusion | flops 51547996160 | bytes 75563008 | tf_op jit(solution)/shard_map/grk,gkc->grc/dot_general | solution.py:55
  285.2 0.0 copy-start.1
  285.2 0.0 reduce-scatter.2.cloned.1.call-update
  285.2 0.0 copy-done
  285.2 0.4 fusion.9
  285.6 0.2 copy-done.1
  285.8 0.1 fusion.10
  285.9 0.1 fusion.7
  286.0 0.1 copy.17
  286.1 0.1 fusion.6
  286.3 143.5 %reduce-scatter.2.cloned.1.call-done = f32[8,128,512]{1,2,0:T(8,128)} async-done(((f32[8,512,512]{1,2,0:T(8,128)}), f32[8,128,512]{1,2,0:T(8,128)}) %reduce-scatter.2.cloned.1.call-update) | async-done | bytes 2097168 | tf_op jit(solution)/shard_map/reduce_scatter | solution.py:16
  429.8 2.5 add_divide_fusion
  432.3 1.8 copy.11
  (9 shorter events, 0.1 us)
Async XLA Ops:
  6.5 278.7 %copy-start = (f32[8,128]{1,0:T(8,128)S(1)}, f32[8,128]{1,0:T(8,128)}, u32[]{:S(2)}) copy-start(f32[8,128]{1,0:T(8,128)} %param.9) | copy-start | bytes 12292
  6.5 0.8 copy-start.2
  6.5 0.8 copy-start.3
  6.5 166.3 %all-gather.2.cloned.1.call-start = ((), (), s32[]{:S(2)}) async-start(), calls=%async_computation.1 | async-start | bytes 37748736 | tf_op jit(solution)/shard_map/all_gather | solution.py:57
  7.3 422.6 %reduce-scatter.2.cloned.1.call-start = ((), (), s32[]{:S(2)}) async-start(), calls=%async_computation.2 | async-start | bytes 10485760 | tf_op jit(solution)/shard_map/reduce_scatter | solution.py:16
  285.2 0.7 copy-start.1
Sparse Core Ops, SparseCore 0:
  9.3 163.4 all-gather.1
  285.3 144.4 reduce-scatter.1
where the time goes:
time: 441 us
  waiting for transfers between devices  309 us (70%)
  matrix products  113 us (26%)
  between operations  13.5 us (3%)
    all_gather x1, waiting for transfers between devices, on_device(): lax.all_gather(t_cycle, 'pair', axis=1, tiled=True)  165 us
    reduce_scatter x1, waiting for transfers between devices, reduce_rows(): lax.psum_scatter(partial_value, 'ph', scatter_dimension=1, tiled=True)  144 us
    dot_general x1, matrix products, on_device(): jnp.einsum('grk,gkc->grc', lax.all_gather(t_cycle, 'pair', axis=1, tiled=...  112 us
  transfers between devices with their start and end apart: 2, of which 2 were waited for; matrix products, arithmetic and copies ran while one was open for 0% of the time, Pallas kernels for 0%

commit v1 on v0

--- a/solution.py
+++ b/solution.py
@@ -41,7 +41,6 @@
     mask_pair = lax.dynamic_slice_in_dim(
         live_slot.reshape(IRREPS, PAIRS), ph_index * local_pairs, local_pairs, 1
     )
-    w_masked = w_cycle * mask_pair[:, :, None]
     mask_row = lax.dynamic_slice_in_dim(
         live_slot[:, :ROW_OCC].reshape(IRREPS, ROWS), ph_index * out_rows, out_rows, 1
     )
@@ -52,14 +51,22 @@
     e_col = (occ_energy[None, :COL_OCC, None] - vir_ener[:, :COL_OCC]).reshape(IRREPS, COLS)
     e_row = lax.dynamic_slice_in_dim(e_row, ph_index * out_rows, out_rows, 1)
     e_col = lax.dynamic_slice_in_dim(e_col, pair_index * local_cols, local_cols, 1)
-    partial_value = jnp.einsum(
-        "grk,gkc->grc",
-        lax.all_gather(t_cycle, "pair", axis=1, tiled=True),
-        w_masked,
-        precision=lax.Precision.HIGHEST,
-        preferred_element_type=jnp.float32,
-    )
-    summed = reduce_rows(partial_value)
+    step = max(1, IRREPS // 4)
+    gathered = [
+        lax.all_gather(t_cycle[first : first + step], "pair", axis=1, tiled=True)
+        for first in range(0, IRREPS, step)
+    ]
+    pieces = []
+    for first, rows in zip(range(0, IRREPS, step), gathered):
+        partial_value = jnp.einsum(
+            "grk,gkc->grc",
+            rows,
+            w_cycle[first : first + step] * mask_pair[first : first + step, :, None],
+            precision=lax.Precision.HIGH,
+            preferred_element_type=jnp.float32,
+        )
+        pieces.append(reduce_rows(partial_value))
+    summed = jnp.concatenate(pieces, axis=0)
     return (
         mask_row[:, :, None]
         * mask_col[:, None, :]

time: 441 us -> 432 us (0.980)
  matrix products: 113 us -> 81.2 us
  waiting for transfers between devices: 309 us -> 326 us
    dot_general x1 -> x4, matrix products: 112 us -> 80.8 us  [on_device(): jnp.einsum('grk,gkc->grc', rows, w_cycle[first:first + step] * mask_pair[...]
    reduce_scatter x1 -> x4, waiting for transfers between devices: 144 us -> 162 us  [reduce_rows(): lax.psum_scatter(partial_value, 'ph', scatter_dimension=1, tiled=True)]
    slice x0 -> x2, local copies, waits for them, and re-layouts: none -> 4.42 us  [the longest x1 4.39 us: on_device(): t_cycle[first:first + step]]
    all_gather x1 -> x4, waiting for transfers between devices: 165 us -> 162 us  [on_device(): lax.all_gather(t_cycle[first:first + step], 'pair', axis=1, tiled=True)]
  transfers between devices with their start and end apart: 2 -> 8, of which waited for: 2 -> 8; matrix products, arithmetic and copies ran while one was open for 0% -> 19% of each run, Pallas kernels for 0% -> 0%
where the time goes in v1:
time: 432 us
  waiting for transfers between devices  326 us (75%)
  matrix products  81.2 us (19%)
  between operations  13.7 us (3%)
  local copies, waits for them, and re-layouts  6.59 us (2%)
    all_gather x4, waiting for transfers between devices, on_device(): lax.all_gather(t_cycle[first:first + step], 'pair', axis=1, tiled=True)  162 us
    reduce_scatter x4, waiting for transfers between devices, reduce_rows(): lax.psum_scatter(partial_value, 'ph', scatter_dimension=1, tiled=True)  162 us
    dot_general x4, matrix products, on_device(): jnp.einsum('grk,gkc->grc', rows, w_cycle[first:first + step] * mask_pair[...  80.8 us
  transfers between devices with their start and end apart: 8, of which 8 were waited for; matrix products, arithmetic and copies ran while one was open for 19% of the time, Pallas kernels for 0%

profile of v1, /device:TPU:0, one launch (start us, length us, event | category | flops | bytes accessed | tf_op | source)
XLA Modules:
  0.0 431.6 jit_solution(280554858822031936)
XLA Ops:
  6.5 0.0 copy-start
  6.5 0.0 copy-start.2
  6.5 0.0 copy-start.3
  6.5 0.0 all-gather.5.cloned.1.call-start
  6.5 4.4 %fusion.36 = (f32[2,64,2048]{2,1,0:T(8,128)}, f32[2,64,2048]{2,1,0:T(8,128)}, f32[2,64,2048]{2,1,0:T(8,128)}, f32[2,64,2048]{2,1,0:T(8,128)}) fusion(f32[8,64,2048]{2,1,0:T(8,128)} %param.6), kind=kLoop, calls=%fused_computation.46 | loop fusion | bytes 8388608 | tf_op jit(solution)/shard_map/slice | solution.py:56
  10.9 0.0 all-gather.5.cloned.1.call-update
  11.0 0.0 all-gather.7.cloned.1.call-start
  11.0 0.7 all-gather.7.cloned.1.call-update
  11.7 0.0 all-gather.9.cloned.1.call-start
  11.8 0.7 all-gather.9.cloned.1.call-update
  12.4 0.0 all-gather.11.cloned.1.call-start
  12.5 0.5 all-gather.11.cloned.1.call-update
  13.0 0.0 reduce-scatter.5.cloned.1.call-start
  13.1 0.0 copy-done.2
  13.1 0.0 copy-done.3
  13.1 0.1 select_reduce_fusion
  13.2 0.1 copy.12
  13.3 0.1 broadcast_bitcast_fusion
  13.5 54.7 %all-gather.5.cloned.1.call-done = f32[2,512,2048]{2,1,0:T(8,128)} async-done(((f32[2,64,2048]{2,1,0:T(8,128)}), f32[2,512,2048]{2,1,0:T(8,128)}) %all-gather.5.cloned.1.call-update) | async-done | bytes 8388624 | tf_op jit(solution)/shard_map/all_gather | solution.py:56
  68.2 20.2 %fusion.17 = f32[2,512,512]{1,2,0:T(8,128)} fusion(f32[2,512,2048]{2,1,0:T(8,128)} %all-gather.5.cloned.1.call-done, f32[8,2048,512]{2,1,0:T(8,128)} %param.7, f32[2,2048]{1,0:T(2,128)S(1)} %get-tuple-element.9), kind=kOutput, calls=%fused_computation.18 | convolution fusion | flops 6444548096 | bytes 18890752 | tf_op jit(solution)/shard_map/grk,gkc->grc/dot_general | solution.py:61
  88.4 0.0 reduce-scatter.5.cloned.1.call-update
  88.4 0.2 reduce-scatter.7.cloned.1.call-start
  88.7 35.9 %all-gather.7.cloned.1.call-done = f32[2,512,2048]{2,1,0:T(8,128)} async-done(((f32[2,64,2048]{2,1,0:T(8,128)}), f32[2,512,2048]{2,1,0:T(8,128)}) %all-gather.7.cloned.1.call-update) | async-done | bytes 8388624 | tf_op jit(solution)/shard_map/all_gather | solution.py:56
  124.5 20.2 %fusion.20 = f32[2,512,512]{1,2,0:T(8,128)} fusion(f32[2,512,2048]{2,1,0:T(8,128)} %all-gather.7.cloned.1.call-done, f32[8,2048,512]{2,1,0:T(8,128)} %param.7, f32[2,2048]{1,0:T(2,128)S(1)} %get-tuple-element.11), kind=kOutput, calls=%fused_computation.19 | convolution fusion | flops 6444548096 | bytes 18890752 | tf_op jit(solution)/shard_map/grk,gkc->grc/dot_general | solution.py:61
  144.7 0.0 reduce-scatter.7.cloned.1.call-update
  144.8 0.3 reduce-scatter.9.cloned.1.call-start
  145.0 35.9 %all-gather.9.cloned.1.call-done = f32[2,512,2048]{2,1,0:T(8,128)} async-done(((f32[2,64,2048]{2,1,0:T(8,128)}), f32[2,512,2048]{2,1,0:T(8,128)}) %all-gather.9.cloned.1.call-update) | async-done | bytes 8388624 | tf_op jit(solution)/shard_map/all_gather | solution.py:56
  180.9 20.2 %fusion.23 = f32[2,512,512]{1,2,0:T(8,128)} fusion(f32[2,512,2048]{2,1,0:T(8,128)} %all-gather.9.cloned.1.call-done, f32[8,2048,512]{2,1,0:T(8,128)} %param.7, f32[2,2048]{1,0:T(2,128)S(1)} %get-tuple-element.10), kind=kOutput, calls=%fused_computation.20 | convolution fusion | flops 6444548096 | bytes 18890752 | tf_op jit(solution)/shard_map/grk,gkc->grc/dot_general | solution.py:61
  201.1 0.0 reduce-scatter.9.cloned.1.call-update
  201.1 0.3 reduce-scatter.11.cloned.1.call-start
  201.4 35.7 %all-gather.11.cloned.1.call-done = f32[2,512,2048]{2,1,0:T(8,128)} async-done(((f32[2,64,2048]{2,1,0:T(8,128)}), f32[2,512,2048]{2,1,0:T(8,128)}) %all-gather.11.cloned.1.call-update) | async-done | bytes 8388624 | tf_op jit(solution)/shard_map/all_gather | solution.py:56
  237.1 0.0 copy-start.1
  237.1 20.2 %fusion.26 = f32[2,512,512]{1,2,0:T(8,128)} fusion(f32[2,512,2048]{2,1,0:T(8,128)} %all-gather.11.cloned.1.call-done, f32[8,2048,512]{2,1,0:T(8,128)} %param.7, f32[2,2048]{1,0:T(2,128)S(1)} %get-tuple-element.12), kind=kOutput, calls=%fused_computation.21 | convolution fusion | flops 6444548096 | bytes 18890752 | tf_op jit(solution)/shard_map/grk,gkc->grc/dot_general | solution.py:61
  257.3 0.0 reduce-scatter.11.cloned.1.call-update
  257.3 0.0 copy-done
  257.3 0.4 fusion.32
  257.7 0.0 copy-done.1
  257.7 0.1 fusion.33
  257.8 0.1 fusion.30
  257.9 0.1 copy.26
  258.0 0.1 fusion.29
  258.2 24.9 %reduce-scatter.5.cloned.1.call-done = f32[2,128,512]{1,2,0:T(8,128)} async-done(((f32[2,512,512]{1,2,0:T(8,128)}), f32[2,128,512]{1,2,0:T(8,128)}) %reduce-scatter.5.cloned.1.call-update) | async-done | bytes 524304 | tf_op jit(solution)/shard_map/reduce_scatter | solution.py:16
  283.1 45.5 %reduce-scatter.7.cloned.1.call-done = f32[2,128,512]{1,2,0:T(8,128)} async-done(((f32[2,512,512]{1,2,0:T(8,128)}), f32[2,128,512]{1,2,0:T(8,128)}) %reduce-scatter.7.cloned.1.call-update) | async-done | bytes 524304 | tf_op jit(solution)/shard_map/reduce_scatter | solution.py:16
  328.6 45.5 %reduce-scatter.9.cloned.1.call-done = f32[2,128,512]{1,2,0:T(8,128)} async-done(((f32[2,512,512]{1,2,0:T(8,128)}), f32[2,128,512]{1,2,0:T(8,128)}) %reduce-scatter.9.cloned.1.call-update) | async-done | bytes 524304 | tf_op jit(solution)/shard_map/reduce_scatter | solution.py:16
  374.1 45.6 %reduce-scatter.11.cloned.1.call-done = f32[2,128,512]{1,2,0:T(8,128)} async-done(((f32[2,512,512]{1,2,0:T(8,128)}), f32[2,128,512]{1,2,0:T(8,128)}) %reduce-scatter.11.cloned.1.call-update) | async-done | bytes 524304 | tf_op jit(solution)/shard_map/reduce_scatter | solution.py:16
  419.7 3.3 fusion.16
  422.9 1.8 copy.17
  (10 shorter events, 0.1 us)
Async XLA Ops:
  6.5 250.7 %copy-start = (f32[8,128]{1,0:T(8,128)S(1)}, f32[8,128]{1,0:T(8,128)}, u32[]{:S(2)}) copy-start(f32[8,128]{1,0:T(8,128)} %param.9) | copy-start | bytes 12292
  6.5 6.5 %copy-start.2 = (s32[64]{0:T(128)S(1)}, s32[64]{0:T(128)}, u32[]{:S(2)}) copy-start(s32[64]{0:T(128)} %param.10) | copy-start | bytes 772
  6.5 6.6 %copy-start.3 = (s32[8]{0:T(128)S(1)}, s32[8]{0:T(128)}, u32[]{:S(2)}) copy-start(s32[8]{0:T(128)} %param.11) | copy-start | bytes 100
  6.5 61.7 %all-gather.5.cloned.1.call-start = ((), (), s32[]{:S(2)}) async-start(), calls=%async_computation.4 | async-start | bytes 9437184 | tf_op jit(solution)/shard_map/all_gather | solution.py:56
  11.0 113.6 %all-gather.7.cloned.1.call-start = ((), (), s32[]{:S(2)}) async-start(), calls=%async_computation.6 | async-start | bytes 9437184 | tf_op jit(solution)/shard_map/all_gather | solution.py:56
  11.7 169.2 %all-gather.9.cloned.1.call-start = ((), (), s32[]{:S(2)}) async-start(), calls=%async_computation.8 | async-start | bytes 9437184 | tf_op jit(solution)/shard_map/all_gather | solution.py:56
  12.4 224.6 %all-gather.11.cloned.1.call-start = ((), (), s32[]{:S(2)}) async-start(), calls=%async_computation.10 | async-start | bytes 9437184 | tf_op jit(solution)/shard_map/all_gather | solution.py:56
  13.0 270.1 %reduce-scatter.5.cloned.1.call-start = ((), (), s32[]{:S(2)}) async-start(), calls=%async_computation.5 | async-start | bytes 2621440 | tf_op jit(solution)/shard_map/reduce_scatter | solution.py:16
  88.4 240.1 %reduce-scatter.7.cloned.1.call-start = ((), (), s32[]{:S(2)}) async-start(), calls=%async_computation.7 | async-start | bytes 2621440 | tf_op jit(solution)/shard_map/reduce_scatter | solution.py:16
  144.8 229.3 %reduce-scatter.9.cloned.1.call-start = ((), (), s32[]{:S(2)}) async-start(), calls=%async_computation.9 | async-start | bytes 2621440 | tf_op jit(solution)/shard_map/reduce_scatter | solution.py:16
  201.1 218.6 %reduce-scatter.11.cloned.1.call-start = ((), (), s32[]{:S(2)}) async-start(), calls=%async_computation.11 | async-start | bytes 2621440 | tf_op jit(solution)/shard_map/reduce_scatter | solution.py:16
  237.1 20.6 %copy-start.1 = (f32[64]{0:T(128)S(1)}, f32[64]{0:T(128)}, u32[]{:S(2)}) copy-start(f32[64]{0:T(128)} %param.8) | copy-start | bytes 772
Sparse Core Ops, SparseCore 0:
  11.1 57.0 all-gather.4
  70.1 54.3 all-gather.6
  126.4 54.3 all-gather.8
  182.6 54.3 all-gather.10
  239.2 43.8 reduce-scatter.4
  285.3 43.1 reduce-scatter.6
  330.9 43.1 reduce-scatter.8
  376.5 43.1 reduce-scatter.10

commit v2 on v0

v2 whole, which is shorter than its diff:
```python
import functools

import jax
import jax.numpy as jnp
from jax import lax
from jax.experimental import pallas as pl
from jax.experimental.pallas import tpu as pltpu
from jax.sharding import PartitionSpec as P

IRREPS = 8
VIRT_CAP = 128
VIRTUALS = 640
ROW_OCC = 4
CHUNKS = 5
VMEM_LIMIT = 56 * 1024 * 1024


def offsets_of(count_ref):
    offs = [jnp.int32(0)]
    for h in range(IRREPS):
        offs.append(offs[-1] + count_ref[h])
    return offs


def pick(values, index):
    result = values[0]
    for position in range(1, len(values)):
        result = jnp.where(index == position, values[position], result)
    return result


def split_kernel(irrep_ref, count_ref, w_ref, hi_ref, lo_ref):
    g = pl.program_id(0)
    tile = w_ref.shape[1]
    per_tile = tile // VIRT_CAP
    first = (lax.axis_index("ph") * pl.num_programs(1) + pl.program_id(1)) * per_tile
    slot = lax.broadcasted_iota(jnp.int32, (VIRT_CAP, w_ref.shape[2]), 0)
    for k in range(per_tile):
        live = slot < count_ref[jnp.bitwise_xor(irrep_ref[first + k], g)]
        rows = pl.ds(k * VIRT_CAP, VIRT_CAP)
        value = jnp.where(live, w_ref[0, rows, :], 0.0)
        high = value.astype(jnp.bfloat16)
        hi_ref[0, rows, :] = high
        lo_ref[0, rows, :] = (value - high.astype(jnp.float32)).astype(jnp.bfloat16)


def split_weights(occ_irrep, vir_count, w):
    irreps, pairs, cols = w.shape
    tile = min(pairs, 1024)
    spec = pl.BlockSpec((1, tile, cols), lambda g, p, *_: (g, p, 0))
    part = jax.ShapeDtypeStruct(w.shape, jnp.bfloat16)
    return pl.pallas_call(
        split_kernel,
        out_shape=(part, part),
        grid_spec=pltpu.PrefetchScalarGridSpec(
            num_scalar_prefetch=2, grid=(irreps, pairs // tile), in_specs=[spec], out_specs=[spec, spec]
        ),
        compiler_params=pltpu.CompilerParams(vmem_limit_bytes=VMEM_LIMIT),
        cost_estimate=pl.CostEstimate(flops=4 * w.size, bytes_accessed=8 * w.size, transcendentals=0),
    )(occ_irrep, vir_count, w)


def compact_kernel(group, irrep_ref, count_ref, *refs):
    parts, outs = refs[:group], refs[group:]
    me = lax.axis_index("pair")
    sub, i = lax.rem(me, group), lax.div(me, group)
    local = parts[0].shape[1]
    half = outs[0].shape[0]
    offs = offsets_of(count_ref)
    irrep = irrep_ref[i]
    for piece, out in enumerate(outs):
        start = (piece // 2) * (2 * half * group) + sub * (2 * half) + (piece % 2) * half

        @pl.loop(0, half, unroll=4)
        def _(r, out=out, start=start):
            v = start + r
            h, base = jnp.int32(0), jnp.int32(0)
            for m in range(1, IRREPS):
                past = offs[m] <= v
                h = jnp.where(past, m, h)
                base = jnp.where(past, offs[m], base)
            a = v - base
            g = jnp.bitwise_xor(irrep, h)
            owner, row = jnp.bitwise_xor(lax.div(a, local), sub), lax.rem(a, local)
            if group == 2:
                out[pl.ds(r, 1), :] = jnp.where(
                    owner == 0, parts[0][g, pl.ds(row, 1), :], parts[1][g, pl.ds(row, 1), :]
                )
            else:
                for m in range(group):

                    @pl.when(owner == m)
                    def _(m=m):
                        out[pl.ds(r, 1), :] = parts[m][g, pl.ds(row, 1), :]


def compact_rows(occ_irrep, vir_count, parts):
    group = len(parts)
    half = VIRTUALS // (CHUNKS * group * 2)
    pairs = parts[0].shape[2]
    vmem = pl.BlockSpec(memory_space=pltpu.VMEM)
    smem = pl.BlockSpec(memory_space=pltpu.SMEM)
    return pl.pallas_call(
        functools.partial(compact_kernel, group),
        out_shape=[jax.ShapeDtypeStruct((half, pairs), jnp.float32)] * (2 * CHUNKS),
        in_specs=[smem, smem] + [vmem] * group,
        out_specs=[vmem] * (2 * CHUNKS),
        compiler_params=pltpu.CompilerParams(vmem_limit_bytes=VMEM_LIMIT),
    )(occ_irrep, vir_count, *parts)


def product_kernel(group, chunk, irrep_ref, count_ref, *refs):
    n_parts = 2 * group * ROW_OCC
    parts, (whi_ref, wlo_ref, out_ref, rows_ref, both_ref) = refs[:n_parts], refs[n_parts:]
    i, h = pl.program_id(0), pl.program_id(1)
    me = lax.axis_index("pair")
    sub, mine = lax.rem(me, group), lax.div(me, group)
    half = parts[0].shape[0]
    rows = rows_ref.shape[0]

    @pl.when(h == 0)
    def _():
        for q in range(ROW_OCC):

            @pl.when(jnp.bitwise_xor(i, mine) == q)
            def _(q=q):
                for c in range(group):
                    at = jnp.bitwise_xor(sub, c) * (2 * half)
                    for side in range(2):
                        rows_ref[pl.ds(pl.multiple_of(at + side * half, 8), half), :] = parts[
                            (q * group + c) * 2 + side
                        ][...]

        value = rows_ref[...]
        high = value.astype(jnp.bfloat16)
        both_ref[:rows, :] = high
        both_ref[rows:, :] = (value - high.astype(jnp.float32)).astype(jnp.bfloat16)
        out_ref[...] = jnp.zeros_like(out_ref)

    offs = offsets_of(count_ref)
    low, top = pick(offs[:-1], h) - chunk * rows, pick(offs[1:], h) - chunk * rows

    @pl.when((low < rows) & (top > 0))
    def _():
        first = jnp.dot(both_ref[...], whi_ref[0], preferred_element_type=jnp.float32)
        second = jnp.dot(both_ref[:rows, :], wlo_ref[0], preferred_element_type=jnp.float32)
        total = first[:rows] + (first[rows:] + second)
        row = lax.broadcasted_iota(jnp.int32, total.shape, 0)
        out_ref[0] = jnp.where((row >= low) & (row < top), total, out_ref[0])


def product(occ_irrep, vir_count, chunk, parts, w_hi, w_lo, group):
    rows = VIRTUALS // CHUNKS
    irreps, pairs, cols = w_hi.shape

    def block_of(i, h, irrep_ref, count_ref):
        offs = offsets_of(count_ref)
        first, last = jnp.int32(0), jnp.int32(-1)
        for m in range(IRREPS):
            first = first + jnp.where(offs[m + 1] <= chunk * rows, 1, 0)
            last = last + jnp.where(offs[m] < (chunk + 1) * rows, 1, 0)
        return jnp.bitwise_xor(irrep_ref[i], jnp.clip(h, first, last)), 0, 0

    t_spec = pl.BlockSpec(parts[0].shape, lambda i, h, *_: (0, 0), pipeline_mode=pl.Buffered(1))
    w_spec = pl.BlockSpec((1, pairs, cols), block_of)
    out = pl.pallas_call(
        functools.partial(product_kernel, group, chunk),
        out_shape=jax.ShapeDtypeStruct((ROW_OCC, rows, cols), jnp.float32),
        grid_spec=pltpu.PrefetchScalarGridSpec(
            num_scalar_prefetch=2,
            grid=(ROW_OCC, irreps),
            in_specs=[t_spec] * len(parts) + [w_spec, w_spec],
            out_specs=pl.BlockSpec((1, rows, cols), lambda i, h, *_: (i, 0, 0)),
            scratch_shapes=[pltpu.VMEM((rows, pairs), jnp.float32), pltpu.VMEM((2 * rows, pairs), jnp.bfloat16)],
        ),
        compiler_params=pltpu.CompilerParams(vmem_limit_bytes=VMEM_LIMIT),
        cost_estimate=pl.CostEstimate(
            flops=2 * 6 * 2 * ROW_OCC * rows * pairs * cols, bytes_accessed=40 * 2**20, transcendentals=0
        ),
    )(occ_irrep, vir_count, *parts, w_hi, w_lo)
    return out.reshape(ROW_OCC * rows, cols)


def expand_kernel(share, irrep_ref, count_ref, occ_ref, vir_ref, vir_t_ref, *refs):
    pieces, (out_ref, all_ref) = refs[:CHUNKS], refs[CHUNKS:]
    g = pl.program_id(0)
    ph, pair = lax.axis_index("ph"), lax.axis_index("pair")
    rows = pieces[0].shape[0]
    out_rows, cols = out_ref.shape[1:]

    @pl.when(g == 0)
    def _():
        for s, piece in enumerate(pieces):
            all_ref[s * rows : (s + 1) * rows, :] = piece[...]
        all_ref[CHUNKS * rows :, :] = jnp.zeros_like(all_ref[CHUNKS * rows :, :])

    i, first_slot = lax.div(ph, share), lax.rem(ph, share) * out_rows
    h = jnp.bitwise_xor(irrep_ref[i], g)
    start = jnp.minimum(pick(offsets_of(count_ref)[:-1], h) + first_slot, CHUNKS * rows)
    base = pl.multiple_of(lax.div(start, 8) * 8, 8)
    window = all_ref[pl.ds(base, out_rows + 8), :]
    window = pltpu.roll(window, lax.rem(out_rows + 8 - (start - base), out_rows + 8), 0)[:out_rows]
    lane = lax.broadcasted_iota(jnp.int32, (VIRT_CAP, IRREPS), 1)
    row_slot = lax.broadcasted_iota(jnp.int32, (VIRT_CAP, 1), 0)
    e_row = jnp.sum(jnp.where(lane == h, vir_t_ref[...], 0.0), axis=1, keepdims=True)
    mine = jnp.zeros((out_rows, 1), jnp.float32)
    for position in range(share):
        part = e_row[position * out_rows : (position + 1) * out_rows]
        mine = jnp.where(lax.rem(ph, share) == position, part, mine)
    e_row = occ_ref[i] - mine
    row_slot = first_slot + lax.broadcasted_iota(jnp.int32, (out_rows, VIRT_CAP), 0)
    col_slot = lax.broadcasted_iota(jnp.int32, (out_rows, VIRT_CAP), 1)
    row_live = row_slot < count_ref[h]
    per_device = cols // VIRT_CAP
    for b in range(per_device):
        j = pair * per_device + b
        col_irrep = jnp.bitwise_xor(irrep_ref[j], g)
        e_col = occ_ref[j] - vir_ref[pl.ds(col_irrep, 1), :]
        lanes = slice(b * VIRT_CAP, (b + 1) * VIRT_CAP)
        live = row_live & (col_slot < count_ref[col_irrep])
        out_ref[0, :, lanes] = jnp.where(live, window[:, lanes], 0.0) / (e_row + e_col)


def expand(occ_irrep, vir_count, occ_energy, vir_energy, pieces, out_rows, share):
    cols = pieces[0].shape[1]
    rows = VIRTUALS // CHUNKS
    smem = pl.BlockSpec(memory_space=pltpu.SMEM)

    def whole(array):
        return pl.BlockSpec(array.shape, lambda g: (0,) * array.ndim)

    vir_t = vir_energy.T
    return pl.pallas_call(
        functools.partial(expand_kernel, share),
        out_shape=jax.ShapeDtypeStruct((IRREPS, out_rows, cols), jnp.float32),
        grid=(IRREPS,),
        in_specs=[smem, smem, smem, whole(vir_energy), whole(vir_t)] + [whole(piece) for piece in pieces],
        out_specs=pl.BlockSpec((1, out_rows, cols), lambda g: (g, 0, 0)),
        scratch_shapes=[pltpu.VMEM((CHUNKS * rows + out_rows + 8, cols), jnp.float32)],
        compiler_params=pltpu.CompilerParams(vmem_limit_bytes=VMEM_LIMIT),
    )(occ_irrep, vir_count, occ_energy, vir_energy, vir_t, *pieces)


def on_device(t_cycle, w_cycle, occ_energy, vir_energy, occ_irrep, vir_count):
    n_pair = lax.axis_size("pair")
    n_ph = lax.axis_size("ph")
    group = n_pair // ROW_OCC
    share = n_ph // ROW_OCC
    out_rows = t_cycle.shape[1] * n_pair // n_ph

    def swap(array, bits):
        return lax.ppermute(array, "pair", [(d, d ^ bits) for d in range(n_pair)])

    parts = [t_cycle] + [swap(t_cycle, m) for m in range(1, group)]
    own = compact_rows(occ_irrep, vir_count, parts)
    w_hi, w_lo = split_weights(occ_irrep, vir_count, w_cycle)
    pieces = []
    for s in range(CHUNKS):
        a, b = own[2 * s], own[2 * s + 1]
        near_a, near_b = swap(a, group), swap(b, group)
        far_a, far_b = swap(a, 2 * group), swap(b, 2 * group)
        held = {0: (a, b), 1: (near_a, near_b), 2: (far_a, far_b)}
        held[3] = (swap(near_a, 2 * group), swap(far_b, group))
        rows = []
        for q in range(ROW_OCC):
            for c in range(group):
                rows += [array if c == 0 else swap(array, c) for array in held[q]]
        partial_value = product(occ_irrep, vir_count, s, rows, w_hi, w_lo, group)
        summed = lax.psum_scatter(partial_value, "ph", scatter_dimension=0, tiled=True)
        if share > 1:
            groups = [[i * share + p for p in range(share)] for i in range(ROW_OCC)]
            summed = lax.all_gather(summed, "ph", axis=0, tiled=True, axis_index_groups=groups)
        pieces.append(summed)
    return expand(occ_irrep, vir_count, occ_energy, vir_energy, pieces, out_rows, share)


def solution(mesh):
    return jax.shard_map(
        on_device,
        mesh=mesh,
        in_specs=(P(None, "pair", "ph"), P(None, "ph", "pair"), P(), P(), P(), P()),
        out_specs=P(None, "ph", "pair"),
        check_vma=False,
    )
```

time: 441 us -> 364 us (0.83)
  waiting for transfers between devices: 309 us -> 110 us
  Pallas kernels: 0 us -> 189 us
  matrix products: 113 us -> 0 us
  starting transfers between devices: 0.04 us -> 42.6 us
  local copies, waits for them, and re-layouts: 2.37 us -> 7.77 us
    pallas_call x0 -> x8, Pallas kernels: none -> 189 us  [the longest x5 144 us: product(): pl.pallas_call(functools.partial(product_kernel, group, chunk), out_shape...]
    all_gather x1 -> x0, waiting for transfers between devices: 165 us -> none  [on_device(): lax.all_gather(t_cycle, 'pair', axis=1, tiled=True)]
    reduce_scatter x1 -> x5, waiting for transfers between devices: 144 us -> 27.5 us  [on_device(): lax.psum_scatter(partial_value, 'ph', scatter_dimension=0, tiled=True)]
    dot_general x2 -> x0, matrix products: 113 us -> none  [the longest x1 112 us: on_device(): jnp.einsum('grk,gkc->grc', lax.all_gather(t_cycle, 'pair', axis=1, tiled=...]
    ppermute x0 -> x71, waiting for transfers between devices: none -> 82.6 us  [swap(): return lax.ppermute(array, 'pair', [(d, d ^ bits) for d in range(n_pair)])]
    ppermute x0 -> x71, starting transfers between devices: none -> 42.3 us  [swap(): return lax.ppermute(array, 'pair', [(d, d ^ bits) for d in range(n_pair)])]
    unnamed x10 -> x161, local copies, waits for them, and re-layouts: 0.3 us -> 7.77 us
  transfers between devices with their start and end apart: 2 -> 76, of which waited for: 2 -> 44; matrix products, arithmetic and copies ran while one was open for 0% -> 0% of each run, Pallas kernels for 0% -> 41%
where the time goes in v2:
time: 364 us
  Pallas kernels  189 us (52%)
  waiting for transfers between devices  110 us (30%)
  starting transfers between devices  42.6 us (12%)
  between operations  13.9 us (4%)
  local copies, waits for them, and re-layouts  7.77 us (2%)
    pallas_call x5, Pallas kernels, product(): pl.pallas_call(functools.partial(product_kernel, group, chunk), out_shape...  144 us
    ppermute x71, waiting for transfers between devices, swap(): return lax.ppermute(array, 'pair', [(d, d ^ bits) for d in range(n_pair)])  82.6 us
    ppermute x71, starting transfers between devices, swap(): return lax.ppermute(array, 'pair', [(d, d ^ bits) for d in range(n_pair)])  42.3 us
    pallas_call x1, Pallas kernels, split_weights(): pl.pallas_call(split_kernel, out_shape=(part, part), grid_spec=pltpu.Pref...  29.3 us
    reduce_scatter x5, waiting for transfers between devices, on_device(): lax.psum_scatter(partial_value, 'ph', scatter_dimension=0, tiled=True)  27.5 us
    pallas_call x1, Pallas kernels, compact_rows(): pl.pallas_call(functools.partial(compact_kernel, group), out_shape=[jax.S...  10.9 us
    unnamed x161, local copies, waits for them, and re-layouts  7.77 us
  transfers between devices with their start and end apart: 76, of which 44 were waited for; matrix products, arithmetic and copies ran while one was open for 0% of the time, Pallas kernels for 41%

profile of v2, /device:TPU:0, one launch (start us, length us, event | category | flops | bytes accessed | tf_op | source)
XLA Modules:
  0.0 363.8 jit_solution(7039606764900830193)
XLA Ops:
  7.0 7.0 %collective-permute-done.refs_1_ = f32[8,64,2048]{2,1,0:T(8,128)S(1)} collective-permute-done((f32[8,64,2048]{2,1,0:T(8,128)}, f32[8,64,2048]{2,1,0:T(8,128)S(1)}, u32[]{:S(2)}, u32[]{:S(2)}) %collective-permute-start) | collective-permute-done | bytes 4194336 | tf_op jit(solution)/shard_map/ppermute | solution.py:252
  14.0 2.0 copy-done
  16.0 10.9 %shard_map.64 = (f32[32,2048]{1,0:T(8,128)}, f32[32,2048]{1,0:T(8,128)}, f32[32,2048]{1,0:T(8,128)}, f32[32,2048]{1,0:T(8,128)}, f32[32,2048]{1,0:T(8,128)}, /*i...) custom-call(s32[64]{0:T(128)} %irrep_ref.15, ...), custom_call_target="tpu_custom_call" | custom-call | tf_op jit(solution)/shard_map/pallas_call | solution.py:103
  26.9 2.9 collective-permute-start.59
  29.8 1.5 collective-permute-start.64
  31.8 5.2 %collective-permute-done.59.refs_4_ = f32[32,2048]{1,0:T(8,128)S(1)} collective-permute-done((f32[32,2048]{1,0:T(8,128)}, f32[32,2048]{1,0:T(8,128)S(1)}, u32[]{:S(2)}, u32[]{:S(2)}) %collective-permute-start.59) | collective-permute-done | bytes 262176 | tf_op jit(solution)/shard_map/ppermute | solution.py:252
  37.1 2.1 collective-permute-done.64.refs_9_
  39.2 1.5 collective-permute-start.67
  40.7 1.5 collective-permute-done.60.refs_5_
  42.2 1.7 collective-permute-start.68
  43.9 0.8 collective-permute-done.63.refs_8_
  45.4 3.9 %collective-permute-done.67.refs_12_ = f32[32,2048]{1,0:T(8,128)S(1)} collective-permute-done((f32[32,2048]{1,0:T(8,128)S(1)}, f32[32,2048]{1,0:T(8,128)S(1)}, u32[]{:S(2)}, u32[]{:S(2)}) %collective-permute-start.67) | collective-permute-done | bytes 262176 | tf_op jit(solution)/shard_map/ppermute | solution.py:252
  50.5 29.3 %shard_map.65 = (bf16[8,2048,512]{2,1,0:T(8,128)(2,1)}, bf16[8,2048,512]{2,1,0:T(8,128)(2,1)}) custom-call(s32[64]{0:T(128)} %irrep_ref.15, s32[8]{0:T(128)} %count_ref.15, f32[8,2048,512]{2,1,0:T(8,128)} %w_ref.1), custom_call_target="tpu_custom_call" | custom-call | flops 33554432 | bytes 67108864 | tf_op jit(solution)/shard_map/pallas_call | solution.py:52
  81.0 24.4 %shard_map.70 = f32[4,128,512]{2,1,0:T(8,128)} custom-call(s32[64]{0:T(128)} %irrep_ref.15, s32[8]{0:T(128)} %count_ref.15, f32[32,2048]{1,0:T(8,128)} %get-tuple-element.27.refs_0_, f32[32,2048]{1,0:T(8,128)} %get-tuple-element.28.refs_1_, f32[32,2048]{1,0:T(8,128)} %copy-done.27, f32[32,2048]{1,0:T(8,128)} %copy-done.35, f32[32,2048]{1,0:T(8,128)} %copy-done.10, ...), custom_call_target="tpu_custom_call" | custom-call | flops 12884901888 | bytes 41943040 | tf_op jit(solution)/shard_map/pallas_call | solution.py:166
  105.5 1.5 collective-permute-start.45
  107.0 1.5 collective-permute-start.50
  109.6 5.1 %collective-permute-done.45.refs_4_ = f32[32,2048]{1,0:T(8,128)S(1)} collective-permute-done((f32[32,2048]{1,0:T(8,128)S(1)}, f32[32,2048]{1,0:T(8,128)S(1)}, u32[]{:S(2)}, u32[]{:S(2)}) %collective-permute-start.45) | collective-permute-done | bytes 262176 | tf_op jit(solution)/shard_map/ppermute | solution.py:252
  114.7 1.5 collective-permute-done.50.refs_9_
  116.2 1.5 collective-permute-start.53
  117.7 1.8 collective-permute-done.46.refs_5_
  119.5 1.4 collective-permute-start.54
  120.9 0.9 collective-permute-done.49.refs_8_
  122.4 3.8 %collective-permute-done.53.refs_12_ = f32[32,2048]{1,0:T(8,128)S(1)} collective-permute-done((f32[32,2048]{1,0:T(8,128)S(1)}, f32[32,2048]{1,0:T(8,128)S(1)}, u32[]{:S(2)}, u32[]{:S(2)}) %collective-permute-start.53) | collective-permute-done | bytes 262176 | tf_op jit(solution)/shard_map/ppermute | solution.py:252
  126.2 0.8 collective-permute-done.54.refs_13_
  127.8 0.8 collective-permute-done.55.refs_14_
  130.0 32.5 %shard_map.69 = f32[4,128,512]{2,1,0:T(8,128)} custom-call(s32[64]{0:T(128)} %irrep_ref.15, s32[8]{0:T(128)} %count_ref.15, f32[32,2048]{1,0:T(8,128)} %get-tuple-element.25.refs_0_, f32[32,2048]{1,0:T(8,128)} %get-tuple-element.26.refs_1_, f32[32,2048]{1,0:T(8,128)} %copy-done.32, f32[32,2048]{1,0:T(8,128)} %copy-done.37, f32[32,2048]{1,0:T(8,128)} %copy-done.13, ...), custom_call_target="tpu_custom_call" | custom-call | flops 12884901888 | bytes 41943040 | tf_op jit(solution)/shard_map/pallas_call | solution.py:166
  162.5 1.5 collective-permute-start.31
  164.0 1.5 collective-permute-start.36
  166.7 5.1 %collective-permute-done.31.refs_4_ = f32[32,2048]{1,0:T(8,128)S(1)} collective-permute-done((f32[32,2048]{1,0:T(8,128)S(1)}, f32[32,2048]{1,0:T(8,128)S(1)}, u32[]{:S(2)}, u32[]{:S(2)}) %collective-permute-start.31) | collective-permute-done | bytes 262176 | tf_op jit(solution)/shard_map/ppermute | solution.py:252
  171.8 1.5 collective-permute-done.36.refs_9_
  173.2 1.5 collective-permute-start.39
  174.7 1.9 collective-permute-done.32.refs_5_
  176.6 1.4 collective-permute-start.40
  178.0 0.8 collective-permute-done.35.refs_8_
  179.4 3.9 %collective-permute-done.39.refs_12_ = f32[32,2048]{1,0:T(8,128)S(1)} collective-permute-done((f32[32,2048]{1,0:T(8,128)S(1)}, f32[32,2048]{1,0:T(8,128)S(1)}, u32[]{:S(2)}, u32[]{:S(2)}) %collective-permute-start.39) | collective-permute-done | bytes 262176 | tf_op jit(solution)/shard_map/ppermute | solution.py:252
  183.3 0.9 collective-permute-done.40.refs_13_
  184.9 0.9 collective-permute-done.41.refs_14_
  187.2 29.3 %shard_map.68 = f32[4,128,512]{2,1,0:T(8,128)} custom-call(s32[64]{0:T(128)} %irrep_ref.15, s32[8]{0:T(128)} %count_ref.15, f32[32,2048]{1,0:T(8,128)} %get-tuple-element.23.refs_0_, f32[32,2048]{1,0:T(8,128)} %get-tuple-element.24.refs_1_, f32[32,2048]{1,0:T(8,128)} %copy-done.33, f32[32,2048]{1,0:T(8,128)} %copy-done.38, f32[32,2048]{1,0:T(8,128)} %copy-done.14, ...), custom_call_target="tpu_custom_call" | custom-call | flops 12884901888 | bytes 41943040 | tf_op jit(solution)/shard_map/pallas_call | solution.py:166
  216.7 1.5 collective-permute-start.17
  218.2 1.5 collective-permute-start.22
  220.8 5.1 %collective-permute-done.17.refs_4_ = f32[32,2048]{1,0:T(8,128)S(1)} collective-permute-done((f32[32,2048]{1,0:T(8,128)S(1)}, f32[32,2048]{1,0:T(8,128)S(1)}, u32[]{:S(2)}, u32[]{:S(2)}) %collective-permute-start.17) | collective-permute-done | bytes 262176 | tf_op jit(solution)/shard_map/ppermute | solution.py:252
  225.9 1.5 collective-permute-done.22.refs_9_
  227.4 1.5 collective-permute-start.25
  228.9 1.9 collective-permute-done.18.refs_5_
  230.8 1.4 collective-permute-start.26
  232.2 0.8 collective-permute-done.21.refs_8_
  233.6 3.9 %collective-permute-done.25.refs_12_ = f32[32,2048]{1,0:T(8,128)S(1)} collective-permute-done((f32[32,2048]{1,0:T(8,128)S(1)}, f32[32,2048]{1,0:T(8,128)S(1)}, u32[]{:S(2)}, u32[]{:S(2)}) %collective-permute-start.25) | collective-permute-done | bytes 262176 | tf_op jit(solution)/shard_map/ppermute | solution.py:252
  237.5 0.9 collective-permute-done.26.refs_13_
  239.1 0.9 collective-permute-done.27.refs_14_
  241.3 32.6 %shard_map.67 = f32[4,128,512]{2,1,0:T(8,128)} custom-call(s32[64]{0:T(128)} %irrep_ref.15, s32[8]{0:T(128)} %count_ref.15, f32[32,2048]{1,0:T(8,128)} %get-tuple-element.21.refs_0_, f32[32,2048]{1,0:T(8,128)} %get-tuple-element.22.refs_1_, f32[32,2048]{1,0:T(8,128)} %copy-done.34, f32[32,2048]{1,0:T(8,128)} %copy-done.39, f32[32,2048]{1,0:T(8,128)} %copy-done.15, ...), custom_call_target="tpu_custom_call" | custom-call | flops 12884901888 | bytes 41943040 | tf_op jit(solution)/shard_map/pallas_call | solution.py:166
  274.1 1.5 collective-permute-start.3
  275.5 1.5 collective-permute-start.8
  278.2 5.1 %collective-permute-done.3.refs_4_ = f32[32,2048]{1,0:T(8,128)S(1)} collective-permute-done((f32[32,2048]{1,0:T(8,128)S(1)}, f32[32,2048]{1,0:T(8,128)S(1)}, u32[]{:S(2)}, u32[]{:S(2)}) %collective-permute-start.3) | collective-permute-done | bytes 262176 | tf_op jit(solution)/shard_map/ppermute | solution.py:252
  283.3 1.4 collective-permute-done.8.refs_9_
  284.7 1.5 collective-permute-start.11
  286.2 1.9 collective-permute-done.4.refs_5_
  288.1 1.4 collective-permute-start.12
  289.5 0.8 collective-permute-done.7.refs_8_
  291.0 3.9 %collective-permute-done.11.refs_12_ = f32[32,2048]{1,0:T(8,128)S(1)} collective-permute-done((f32[32,2048]{1,0:T(8,128)S(1)}, f32[32,2048]{1,0:T(8,128)S(1)}, u32[]{:S(2)}, u32[]{:S(2)}) %collective-permute-start.11) | collective-permute-done | bytes 262176 | tf_op jit(solution)/shard_map/ppermute | solution.py:252
  294.9 0.9 collective-permute-done.12.refs_13_
  296.4 0.9 collective-permute-done.13.refs_14_
  298.7 25.2 %shard_map.66 = f32[4,128,512]{2,1,0:T(8,128)} custom-call(s32[64]{0:T(128)} %irrep_ref.15, s32[8]{0:T(128)} %count_ref.15, f32[32,2048]{1,0:T(8,128)} %get-tuple-element.17.refs_0_, f32[32,2048]{1,0:T(8,128)} %get-tuple-element.18.refs_1_, f32[32,2048]{1,0:T(8,128)} %copy-done.31, f32[32,2048]{1,0:T(8,128)} %copy-done.36, f32[32,2048]{1,0:T(8,128)} %copy-done.11, ...), custom_call_target="tpu_custom_call" | custom-call | flops 12884901888 | bytes 41943040 | tf_op jit(solution)/shard_map/pallas_call | solution.py:166
  324.6 27.4 %reduce-scatter.6.cloned.1.call-done.refs_0_ = f32[128,512]{1,0:T(8,128)} async-done(((f32[512,512]{1,0:T(8,128)}), f32[128,512]{1,0:T(8,128)}) %reduce-scatter.6.cloned.1.call-update) | async-done | bytes 262160 | tf_op jit(solution)/shard_map/reduce_scatter | solution.py:269
  352.1 5.2 %shard_map.71 = f32[8,128,512]{2,1,0:T(8,128)} custom-call(s32[64]{0:T(128)} %irrep_ref.15, s32[8]{0:T(128)} %count_ref.15, f32[64]{0:T(128)} %occ_ref.1, f32[8,128]{1,0:T(8,128)} %vir_ref.1, f32[128,8]{1,0:T(8,128)} %bitcast.11, f32[128,512]{1,0:T(8,128)} %reduce-scatter.6.cloned.1.call-done.refs_0_, f32[128,512]{1,0:T(8,128)} %reduce-scatter.8.cloned.1.call-done.refs_1_, ...), custom_call_target="tpu_custom_call" | custom-call | tf_op jit(solution)/shard_map/pallas_call | solution.py:233
  (262 shorter events, 20.1 us)
Async XLA Ops:
  6.5 318.1 %reduce-scatter.14.cloned.1.call-start = ((), (), s32[]{:S(2)}) async-start(), calls=%async_computation.9 | async-start | bytes 1310720 | tf_op jit(solution)/shard_map/reduce_scatter | solution.py:269
  6.5 7.4 %collective-permute-start = (f32[8,64,2048]{2,1,0:T(8,128)}, f32[8,64,2048]{2,1,0:T(8,128)S(1)}, u32[]{:S(2)}, u32[]{:S(2)}) collective-permute-start(f32[8,64,2048]{2,1,0:T(8,128)} %refs_0_.1), channel_id=1, source_target_pairs={{0,4},{4,0},{8,12},{12,8},{16,20},{20,16},{24,28},{28,24},{1,5},{5... | collective-permute-start | bytes 12582920 | tf_op jit(solution)/shard_map/ppermute | solution.py:252
  26.9 10.2 %collective-permute-start.59 = (f32[32,2048]{1,0:T(8,128)}, f32[32,2048]{1,0:T(8,128)S(1)}, u32[]{:S(2)}, u32[]{:S(2)}) collective-permute-start(f32[32,2048]{1,0:T(8,128)} %get-tuple-element.27.refs_0_), channel_id=1, source_target_pairs={{0,8},{4,12},{8,0},{12,4},{16,24},{20,28},{24,16},{28,20},{1,9},{5... | collective-permute-start | bytes 786440 | tf_op jit(solution)/shard_map/ppermute | solution.py:252
  29.8 9.4 %collective-permute-start.64 = (f32[32,2048]{1,0:T(8,128)}, f32[32,2048]{1,0:T(8,128)S(1)}, u32[]{:S(2)}, u32[]{:S(2)}) collective-permute-start(f32[32,2048]{1,0:T(8,128)} %get-tuple-element.28.refs_1_), channel_id=1, source_target_pairs={{0,16},{4,20},{8,24},{12,28},{16,0},{20,4},{24,8},{28,12},{1,17},{... | collective-permute-start | bytes 786440 | tf_op jit(solution)/shard_map/ppermute | solution.py:252
  31.3 10.9 %collective-permute-start.60 = (f32[32,2048]{1,0:T(8,128)}, f32[32,2048]{1,0:T(8,128)S(1)}, u32[]{:S(2)}, u32[]{:S(2)}) collective-permute-start(f32[32,2048]{1,0:T(8,128)} %get-tuple-element.28.refs_1_), channel_id=1, source_target_pairs={{0,8},{4,12},{8,0},{12,4},{16,24},{20,28},{24,16},{28,20},{1,9},{5... | collective-permute-start | bytes 786440 | tf_op jit(solution)/shard_map/ppermute | solution.py:252
  31.8 13.0 %collective-permute-start.63 = (f32[32,2048]{1,0:T(8,128)}, f32[32,2048]{1,0:T(8,128)S(1)}, u32[]{:S(2)}, u32[]{:S(2)}) collective-permute-start(f32[32,2048]{1,0:T(8,128)} %get-tuple-element.27.refs_0_), channel_id=1, source_target_pairs={{0,16},{4,20},{8,24},{12,28},{16,0},{20,4},{24,8},{28,12},{1,17},{... | collective-permute-start | bytes 786440 | tf_op jit(solution)/shard_map/ppermute | solution.py:252
  31.8 12.9 %collective-permute-start.57 = (f32[32,2048]{1,0:T(8,128)}, f32[32,2048]{1,0:T(8,128)S(1)}, u32[]{:S(2)}, u32[]{:S(2)}) collective-permute-start(f32[32,2048]{1,0:T(8,128)} %get-tuple-element.27.refs_0_), channel_id=1, source_target_pairs={{0,4},{4,0},{8,12},{12,8},{16,20},{20,16},{24,28},{28,24},{1,5},{5... | collective-permute-start | bytes 786440 | tf_op jit(solution)/shard_map/ppermute | solution.py:252
  37.1 8.2 %collective-permute-start.58 = (f32[32,2048]{1,0:T(8,128)}, f32[32,2048]{1,0:T(8,128)S(1)}, u32[]{:S(2)}, u32[]{:S(2)}) collective-permute-start(f32[32,2048]{1,0:T(8,128)} %get-tuple-element.28.refs_1_), channel_id=1, source_target_pairs={{0,4},{4,0},{8,12},{12,8},{16,20},{20,16},{24,28},{28,24},{1,5},{5... | collective-permute-start | bytes 786440 | tf_op jit(solution)/shard_map/ppermute | solution.py:252
  39.2 10.1 %collective-permute-start.67 = (f32[32,2048]{1,0:T(8,128)S(1)}, f32[32,2048]{1,0:T(8,128)S(1)}, u32[]{:S(2)}, u32[]{:S(2)}) collective-permute-start(f32[32,2048]{1,0:T(8,128)S(1)} %collective-permute-done.59.refs_4_), channel_id=1, source_target_pairs={{0,16},{4,20},{8,24},{12,28},{16,0},{20,4},{24,8},{28,12},{1,17},{... | collective-permute-start | bytes 786440 | tf_op jit(solution)/shard_map/ppermute | solution.py:252
  42.2 7.8 %collective-permute-start.68 = (f32[32,2048]{1,0:T(8,128)S(1)}, f32[32,2048]{1,0:T(8,128)S(1)}, u32[]{:S(2)}, u32[]{:S(2)}) collective-permute-start(f32[32,2048]{1,0:T(8,128)S(1)} %collective-permute-done.64.refs_9_), channel_id=1, source_target_pairs={{0,8},{4,12},{8,0},{12,4},{16,24},{20,28},{24,16},{28,20},{1,9},{5... | collective-permute-start | bytes 786440 | tf_op jit(solution)/shard_map/ppermute | solution.py:252
  44.8 5.3 %collective-permute-start.61 = (f32[32,2048]{1,0:T(8,128)S(1)}, f32[32,2048]{1,0:T(8,128)S(1)}, u32[]{:S(2)}, u32[]{:S(2)}) collective-permute-start(f32[32,2048]{1,0:T(8,128)S(1)} %collective-permute-done.59.refs_4_), channel_id=1, source_target_pairs={{0,4},{4,0},{8,12},{12,8},{16,20},{20,16},{24,28},{28,24},{1,5},{5... | collective-permute-start | bytes 786440 | tf_op jit(solution)/shard_map/ppermute | solution.py:252
  44.8 35.1 %collective-permute-start.66 = (f32[32,2048]{1,0:T(8,128)S(1)}, f32[32,2048]{1,0:T(8,128)S(1)}, u32[]{:S(2)}, u32[]{:S(2)}) collective-permute-start(f32[32,2048]{1,0:T(8,128)S(1)} %collective-permute-done.64.refs_9_), channel_id=1, source_target_pairs={{0,4},{4,0},{8,12},{12,8},{16,20},{20,16},{24,28},{28,24},{1,5},{5... | collective-permute-start | bytes 786440 | tf_op jit(solution)/shard_map/ppermute | solution.py:252
  45.3 34.6 %collective-permute-start.62 = (f32[32,2048]{1,0:T(8,128)S(1)}, f32[32,2048]{1,0:T(8,128)S(1)}, u32[]{:S(2)}, u32[]{:S(2)}) collective-permute-start(f32[32,2048]{1,0:T(8,128)S(1)} %collective-permute-done.60.refs_5_), channel_id=1, source_target_pairs={{0,4},{4,0},{8,12},{12,8},{16,20},{20,16},{24,28},{28,24},{1,5},{5... | collective-permute-start | bytes 786440 | tf_op jit(solution)/shard_map/ppermute | solution.py:252
  49.3 30.7 %collective-permute-start.65 = (f32[32,2048]{1,0:T(8,128)S(1)}, f32[32,2048]{1,0:T(8,128)S(1)}, u32[]{:S(2)}, u32[]{:S(2)}) collective-permute-start(f32[32,2048]{1,0:T(8,128)S(1)} %collective-permute-done.63.refs_8_), channel_id=1, source_target_pairs={{0,4},{4,0},{8,12},{12,8},{16,20},{20,16},{24,28},{28,24},{1,5},{5... | collective-permute-start | bytes 786440 | tf_op jit(solution)/shard_map/ppermute | solution.py:252
  50.0 30.0 %collective-permute-start.69 = (f32[32,2048]{1,0:T(8,128)S(1)}, f32[32,2048]{1,0:T(8,128)S(1)}, u32[]{:S(2)}, u32[]{:S(2)}) collective-permute-start(f32[32,2048]{1,0:T(8,128)S(1)} %collective-permute-done.67.refs_12_), channel_id=1, source_target_pairs={{0,4},{4,0},{8,12},{12,8},{16,20},{20,16},{24,28},{28,24},{1,5},{5... | collective-permute-start | bytes 786440 | tf_op jit(solution)/shard_map/ppermute | solution.py:252
  50.0 30.0 %collective-permute-start.70 = (f32[32,2048]{1,0:T(8,128)S(1)}, f32[32,2048]{1,0:T(8,128)S(1)}, u32[]{:S(2)}, u32[]{:S(2)}) collective-permute-start(f32[32,2048]{1,0:T(8,128)S(1)} %collective-permute-done.68.refs_13_), channel_id=1, source_target_pairs={{0,4},{4,0},{8,12},{12,8},{16,20},{20,16},{24,28},{28,24},{1,5},{5... | collective-permute-start | bytes 786440 | tf_op jit(solution)/shard_map/ppermute | solution.py:252
  105.4 219.2 %reduce-scatter.12.cloned.1.call-start = ((), (), s32[]{:S(2)}) async-start(), calls=%async_computation.8 | async-start | bytes 1310720 | tf_op jit(solution)/shard_map/reduce_scatter | solution.py:269
  105.5 9.2 %collective-permute-start.45 = (f32[32,2048]{1,0:T(8,128)S(1)}, f32[32,2048]{1,0:T(8,128)S(1)}, u32[]{:S(2)}, u32[]{:S(2)}) collective-permute-start(f32[32,2048]{1,0:T(8,128)S(1)} %copy-done.8), channel_id=1, source_target_pairs={{0,8},{4,12},{8,0},{12,4},{16,24},{20,28},{24,16},{28,20},{1,9},{5... | collective-permute-start | bytes 786440 | tf_op jit(solution)/shard_map/ppermute | solution.py:252
  107.0 9.2 %collective-permute-start.50 = (f32[32,2048]{1,0:T(8,128)S(1)}, f32[32,2048]{1,0:T(8,128)S(1)}, u32[]{:S(2)}, u32[]{:S(2)}) collective-permute-start(f32[32,2048]{1,0:T(8,128)S(1)} %copy-done.9), channel_id=1, source_target_pairs={{0,16},{4,20},{8,24},{12,28},{16,0},{20,4},{24,8},{28,12},{1,17},{... | collective-permute-start | bytes 786440 | tf_op jit(solution)/shard_map/ppermute | solution.py:252
  108.5 11.0 %collective-permute-start.46 = (f32[32,2048]{1,0:T(8,128)S(1)}, f32[32,2048]{1,0:T(8,128)S(1)}, u32[]{:S(2)}, u32[]{:S(2)}) collective-permute-start(f32[32,2048]{1,0:T(8,128)S(1)} %copy-done.9), channel_id=1, source_target_pairs={{0,8},{4,12},{8,0},{12,4},{16,24},{20,28},{24,16},{28,20},{1,9},{5... | collective-permute-start | bytes 786440 | tf_op jit(solution)/shard_map/ppermute | solution.py:252
  109.0 12.8 %collective-permute-start.49 = (f32[32,2048]{1,0:T(8,128)S(1)}, f32[32,2048]{1,0:T(8,128)S(1)}, u32[]{:S(2)}, u32[]{:S(2)}) collective-permute-start(f32[32,2048]{1,0:T(8,128)S(1)} %copy-done.8), channel_id=1, source_target_pairs={{0,16},{4,20},{8,24},{12,28},{16,0},{20,4},{24,8},{28,12},{1,17},{... | collective-permute-start | bytes 786440 | tf_op jit(solution)/shard_map/ppermute | solution.py:252
  109.6 12.2 %collective-permute-start.43 = (f32[32,2048]{1,0:T(8,128)S(1)}, f32[32,2048]{1,0:T(8,128)S(1)}, u32[]{:S(2)}, u32[]{:S(2)}) collective-permute-start(f32[32,2048]{1,0:T(8,128)S(1)} %copy-done.8), channel_id=1, source_target_pairs={{0,4},{4,0},{8,12},{12,8},{16,20},{20,16},{24,28},{28,24},{1,5},{5... | collective-permute-start | bytes 786440 | tf_op jit(solution)/shard_map/ppermute | solution.py:252
  114.7 7.6 %collective-permute-start.44 = (f32[32,2048]{1,0:T(8,128)S(1)}, f32[32,2048]{1,0:T(8,128)S(1)}, u32[]{:S(2)}, u32[]{:S(2)}) collective-permute-start(f32[32,2048]{1,0:T(8,128)S(1)} %copy-done.9), channel_id=1, source_target_pairs={{0,4},{4,0},{8,12},{12,8},{16,20},{20,16},{24,28},{28,24},{1,5},{5... | collective-permute-start | bytes 786440 | tf_op jit(solution)/shard_map/ppermute | solution.py:252
  116.2 10.0 %collective-permute-start.53 = (f32[32,2048]{1,0:T(8,128)S(1)}, f32[32,2048]{1,0:T(8,128)S(1)}, u32[]{:S(2)}, u32[]{:S(2)}) collective-permute-start(f32[32,2048]{1,0:T(8,128)S(1)} %collective-permute-done.45.refs_4_), channel_id=1, source_target_pairs={{0,16},{4,20},{8,24},{12,28},{16,0},{20,4},{24,8},{28,12},{1,17},{... | collective-permute-start | bytes 786440 | tf_op jit(solution)/shard_map/ppermute | solution.py:252
  119.5 7.6 %collective-permute-start.54 = (f32[32,2048]{1,0:T(8,128)S(1)}, f32[32,2048]{1,0:T(8,128)S(1)}, u32[]{:S(2)}, u32[]{:S(2)}) collective-permute-start(f32[32,2048]{1,0:T(8,128)S(1)} %collective-permute-done.50.refs_9_), channel_id=1, source_target_pairs={{0,8},{4,12},{8,0},{12,4},{16,24},{20,28},{24,16},{28,20},{1,9},{5... | collective-permute-start | bytes 786440 | tf_op jit(solution)/shard_map/ppermute | solution.py:252
  121.8 5.2 %collective-permute-start.47 = (f32[32,2048]{1,0:T(8,128)S(1)}, f32[32,2048]{1,0:T(8,128)S(1)}, u32[]{:S(2)}, u32[]{:S(2)}) collective-permute-start(f32[32,2048]{1,0:T(8,128)S(1)} %collective-permute-done.45.refs_4_), channel_id=1, source_target_pairs={{0,4},{4,0},{8,12},{12,8},{16,20},{20,16},{24,28},{28,24},{1,5},{5... | collective-permute-start | bytes 786440 | tf_op jit(solution)/shard_map/ppermute | solution.py:252
  121.8 5.7 %collective-permute-start.52 = (f32[32,2048]{1,0:T(8,128)S(1)}, f32[32,2048]{1,0:T(8,128)S(1)}, u32[]{:S(2)}, u32[]{:S(2)}) collective-permute-start(f32[32,2048]{1,0:T(8,128)S(1)} %collective-permute-done.50.refs_9_), channel_id=1, source_target_pairs={{0,4},{4,0},{8,12},{12,8},{16,20},{20,16},{24,28},{28,24},{1,5},{5... | collective-permute-start | bytes 786440 | tf_op jit(solution)/shard_map/ppermute | solution.py:252
  122.3 5.2 %collective-permute-start.48 = (f32[32,2048]{1,0:T(8,128)S(1)}, f32[32,2048]{1,0:T(8,128)S(1)}, u32[]{:S(2)}, u32[]{:S(2)}) collective-permute-start(f32[32,2048]{1,0:T(8,128)S(1)} %collective-permute-done.46.refs_5_), channel_id=1, source_target_pairs={{0,4},{4,0},{8,12},{12,8},{16,20},{20,16},{24,28},{28,24},{1,5},{5... | collective-permute-start | bytes 786440 | tf_op jit(solution)/shard_map/ppermute | solution.py:252
  162.5 162.2 %reduce-scatter.10.cloned.1.call-start = ((), (), s32[]{:S(2)}) async-start(), calls=%async_computation.7 | async-start | bytes 1310720 | tf_op jit(solution)/shard_map/reduce_scatter | solution.py:269
  162.5 9.2 %collective-permute-start.31 = (f32[32,2048]{1,0:T(8,128)S(1)}, f32[32,2048]{1,0:T(8,128)S(1)}, u32[]{:S(2)}, u32[]{:S(2)}) collective-permute-start(f32[32,2048]{1,0:T(8,128)S(1)} %copy-done.6), channel_id=1, source_target_pairs={{0,8},{4,12},{8,0},{12,4},{16,24},{20,28},{24,16},{28,20},{1,9},{5... | collective-permute-start | bytes 786440 | tf_op jit(solution)/shard_map/ppermute | solution.py:252
  164.0 9.2 %collective-permute-start.36 = (f32[32,2048]{1,0:T(8,128)S(1)}, f32[32,2048]{1,0:T(8,128)S(1)}, u32[]{:S(2)}, u32[]{:S(2)}) collective-permute-start(f32[32,2048]{1,0:T(8,128)S(1)} %copy-done.7), channel_id=1, source_target_pairs={{0,16},{4,20},{8,24},{12,28},{16,0},{20,4},{24,8},{28,12},{1,17},{... | collective-permute-start | bytes 786440 | tf_op jit(solution)/shard_map/ppermute | solution.py:252
  165.5 11.0 %collective-permute-start.32 = (f32[32,2048]{1,0:T(8,128)S(1)}, f32[32,2048]{1,0:T(8,128)S(1)}, u32[]{:S(2)}, u32[]{:S(2)}) collective-permute-start(f32[32,2048]{1,0:T(8,128)S(1)} %copy-done.7), channel_id=1, source_target_pairs={{0,8},{4,12},{8,0},{12,4},{16,24},{20,28},{24,16},{28,20},{1,9},{5... | collective-permute-start | bytes 786440 | tf_op jit(solution)/shard_map/ppermute | solution.py:252
  166.1 12.8 %collective-permute-start.35 = (f32[32,2048]{1,0:T(8,128)S(1)}, f32[32,2048]{1,0:T(8,128)S(1)}, u32[]{:S(2)}, u32[]{:S(2)}) collective-permute-start(f32[32,2048]{1,0:T(8,128)S(1)} %copy-done.6), channel_id=1, source_target_pairs={{0,16},{4,20},{8,24},{12,28},{16,0},{20,4},{24,8},{28,12},{1,17},{... | collective-permute-start | bytes 786440 | tf_op jit(solution)/shard_map/ppermute | solution.py:252
  166.7 12.2 %collective-permute-start.29 = (f32[32,2048]{1,0:T(8,128)S(1)}, f32[32,2048]{1,0:T(8,128)S(1)}, u32[]{:S(2)}, u32[]{:S(2)}) collective-permute-start(f32[32,2048]{1,0:T(8,128)S(1)} %copy-done.6), channel_id=1, source_target_pairs={{0,4},{4,0},{8,12},{12,8},{16,20},{20,16},{24,28},{28,24},{1,5},{5... | collective-permute-start | bytes 786440 | tf_op jit(solution)/shard_map/ppermute | solution.py:252
  171.7 7.6 %collective-permute-start.30 = (f32[32,2048]{1,0:T(8,128)S(1)}, f32[32,2048]{1,0:T(8,128)S(1)}, u32[]{:S(2)}, u32[]{:S(2)}) collective-permute-start(f32[32,2048]{1,0:T(8,128)S(1)} %copy-done.7), channel_id=1, source_target_pairs={{0,4},{4,0},{8,12},{12,8},{16,20},{20,16},{24,28},{28,24},{1,5},{5... | collective-permute-start | bytes 786440 | tf_op jit(solution)/shard_map/ppermute | solution.py:252
  173.2 10.1 %collective-permute-start.39 = (f32[32,2048]{1,0:T(8,128)S(1)}, f32[32,2048]{1,0:T(8,128)S(1)}, u32[]{:S(2)}, u32[]{:S(2)}) collective-permute-start(f32[32,2048]{1,0:T(8,128)S(1)} %collective-permute-done.31.refs_4_), channel_id=1, source_target_pairs={{0,16},{4,20},{8,24},{12,28},{16,0},{20,4},{24,8},{28,12},{1,17},{... | collective-permute-start | bytes 786440 | tf_op jit(solution)/shard_map/ppermute | solution.py:252
  176.6 7.6 %collective-permute-start.40 = (f32[32,2048]{1,0:T(8,128)S(1)}, f32[32,2048]{1,0:T(8,128)S(1)}, u32[]{:S(2)}, u32[]{:S(2)}) collective-permute-start(f32[32,2048]{1,0:T(8,128)S(1)} %collective-permute-done.36.refs_9_), channel_id=1, source_target_pairs={{0,8},{4,12},{8,0},{12,4},{16,24},{20,28},{24,16},{28,20},{1,9},{5... | collective-permute-start | bytes 786440 | tf_op jit(solution)/shard_map/ppermute | solution.py:252
  178.8 5.4 %collective-permute-start.33 = (f32[32,2048]{1,0:T(8,128)S(1)}, f32[32,2048]{1,0:T(8,128)S(1)}, u32[]{:S(2)}, u32[]{:S(2)}) collective-permute-start(f32[32,2048]{1,0:T(8,128)S(1)} %collective-permute-done.31.refs_4_), channel_id=1, source_target_pairs={{0,4},{4,0},{8,12},{12,8},{16,20},{20,16},{24,28},{28,24},{1,5},{5... | collective-permute-start | bytes 786440 | tf_op jit(solution)/shard_map/ppermute | solution.py:252
  178.8 5.9 %collective-permute-start.38 = (f32[32,2048]{1,0:T(8,128)S(1)}, f32[32,2048]{1,0:T(8,128)S(1)}, u32[]{:S(2)}, u32[]{:S(2)}) collective-permute-start(f32[32,2048]{1,0:T(8,128)S(1)} %collective-permute-done.36.refs_9_), channel_id=1, source_target_pairs={{0,4},{4,0},{8,12},{12,8},{16,20},{20,16},{24,28},{28,24},{1,5},{5... | collective-permute-start | bytes 786440 | tf_op jit(solution)/shard_map/ppermute | solution.py:252
  179.3 5.4 %collective-permute-start.34 = (f32[32,2048]{1,0:T(8,128)S(1)}, f32[32,2048]{1,0:T(8,128)S(1)}, u32[]{:S(2)}, u32[]{:S(2)}) collective-permute-start(f32[32,2048]{1,0:T(8,128)S(1)} %collective-permute-done.32.refs_5_), channel_id=1, source_target_pairs={{0,4},{4,0},{8,12},{12,8},{16,20},{20,16},{24,28},{28,24},{1,5},{5... | collective-permute-start | bytes 786440 | tf_op jit(solution)/shard_map/ppermute | solution.py:252
  216.5 108.2 %reduce-scatter.8.cloned.1.call-start = ((), (), s32[]{:S(2)}) async-start(), calls=%async_computation.6 | async-start | bytes 1310720 | tf_op jit(solution)/shard_map/reduce_scatter | solution.py:269
  216.7 9.2 %collective-permute-start.17 = (f32[32,2048]{1,0:T(8,128)S(1)}, f32[32,2048]{1,0:T(8,128)S(1)}, u32[]{:S(2)}, u32[]{:S(2)}) collective-permute-start(f32[32,2048]{1,0:T(8,128)S(1)} %copy-done.4), channel_id=1, source_target_pairs={{0,8},{4,12},{8,0},{12,4},{16,24},{20,28},{24,16},{28,20},{1,9},{5... | collective-permute-start | bytes 786440 | tf_op jit(solution)/shard_map/ppermute | solution.py:252
  218.2 9.2 %collective-permute-start.22 = (f32[32,2048]{1,0:T(8,128)S(1)}, f32[32,2048]{1,0:T(8,128)S(1)}, u32[]{:S(2)}, u32[]{:S(2)}) collective-permute-start(f32[32,2048]{1,0:T(8,128)S(1)} %copy-done.5), channel_id=1, source_target_pairs={{0,16},{4,20},{8,24},{12,28},{16,0},{20,4},{24,8},{28,12},{1,17},{... | collective-permute-start | bytes 786440 | tf_op jit(solution)/shard_map/ppermute | solution.py:252
  219.7 11.0 %collective-permute-start.18 = (f32[32,2048]{1,0:T(8,128)S(1)}, f32[32,2048]{1,0:T(8,128)S(1)}, u32[]{:S(2)}, u32[]{:S(2)}) collective-permute-start(f32[32,2048]{1,0:T(8,128)S(1)} %copy-done.5), channel_id=1, source_target_pairs={{0,8},{4,12},{8,0},{12,4},{16,24},{20,28},{24,16},{28,20},{1,9},{5... | collective-permute-start | bytes 786440 | tf_op jit(solution)/shard_map/ppermute | solution.py:252
  220.3 12.8 %collective-permute-start.21 = (f32[32,2048]{1,0:T(8,128)S(1)}, f32[32,2048]{1,0:T(8,128)S(1)}, u32[]{:S(2)}, u32[]{:S(2)}) collective-permute-start(f32[32,2048]{1,0:T(8,128)S(1)} %copy-done.4), channel_id=1, source_target_pairs={{0,16},{4,20},{8,24},{12,28},{16,0},{20,4},{24,8},{28,12},{1,17},{... | collective-permute-start | bytes 786440 | tf_op jit(solution)/shard_map/ppermute | solution.py:252
  220.8 12.2 %collective-permute-start.15 = (f32[32,2048]{1,0:T(8,128)S(1)}, f32[32,2048]{1,0:T(8,128)S(1)}, u32[]{:S(2)}, u32[]{:S(2)}) collective-permute-start(f32[32,2048]{1,0:T(8,128)S(1)} %copy-done.4), channel_id=1, source_target_pairs={{0,4},{4,0},{8,12},{12,8},{16,20},{20,16},{24,28},{28,24},{1,5},{5... | collective-permute-start | bytes 786440 | tf_op jit(solution)/shard_map/ppermute | solution.py:252
  225.9 7.6 %collective-permute-start.16 = (f32[32,2048]{1,0:T(8,128)S(1)}, f32[32,2048]{1,0:T(8,128)S(1)}, u32[]{:S(2)}, u32[]{:S(2)}) collective-permute-start(f32[32,2048]{1,0:T(8,128)S(1)} %copy-done.5), channel_id=1, source_target_pairs={{0,4},{4,0},{8,12},{12,8},{16,20},{20,16},{24,28},{28,24},{1,5},{5... | collective-permute-start | bytes 786440 | tf_op jit(solution)/shard_map/ppermute | solution.py:252
  227.4 10.1 %collective-permute-start.25 = (f32[32,2048]{1,0:T(8,128)S(1)}, f32[32,2048]{1,0:T(8,128)S(1)}, u32[]{:S(2)}, u32[]{:S(2)}) collective-permute-start(f32[32,2048]{1,0:T(8,128)S(1)} %collective-permute-done.17.refs_4_), channel_id=1, source_target_pairs={{0,16},{4,20},{8,24},{12,28},{16,0},{20,4},{24,8},{28,12},{1,17},{... | collective-permute-start | bytes 786440 | tf_op jit(solution)/shard_map/ppermute | solution.py:252
  230.8 7.6 %collective-permute-start.26 = (f32[32,2048]{1,0:T(8,128)S(1)}, f32[32,2048]{1,0:T(8,128)S(1)}, u32[]{:S(2)}, u32[]{:S(2)}) collective-permute-start(f32[32,2048]{1,0:T(8,128)S(1)} %collective-permute-done.22.refs_9_), channel_id=1, source_target_pairs={{0,8},{4,12},{8,0},{12,4},{16,24},{20,28},{24,16},{28,20},{1,9},{5... | collective-permute-start | bytes 786440 | tf_op jit(solution)/shard_map/ppermute | solution.py:252
  233.0 5.4 %collective-permute-start.19 = (f32[32,2048]{1,0:T(8,128)S(1)}, f32[32,2048]{1,0:T(8,128)S(1)}, u32[]{:S(2)}, u32[]{:S(2)}) collective-permute-start(f32[32,2048]{1,0:T(8,128)S(1)} %collective-permute-done.17.refs_4_), channel_id=1, source_target_pairs={{0,4},{4,0},{8,12},{12,8},{16,20},{20,16},{24,28},{28,24},{1,5},{5... | collective-permute-start | bytes 786440 | tf_op jit(solution)/shard_map/ppermute | solution.py:252
  233.0 5.9 %collective-permute-start.24 = (f32[32,2048]{1,0:T(8,128)S(1)}, f32[32,2048]{1,0:T(8,128)S(1)}, u32[]{:S(2)}, u32[]{:S(2)}) collective-permute-start(f32[32,2048]{1,0:T(8,128)S(1)} %collective-permute-done.22.refs_9_), channel_id=1, source_target_pairs={{0,4},{4,0},{8,12},{12,8},{16,20},{20,16},{24,28},{28,24},{1,5},{5... | collective-permute-start | bytes 786440 | tf_op jit(solution)/shard_map/ppermute | solution.py:252
  233.5 5.4 %collective-permute-start.20 = (f32[32,2048]{1,0:T(8,128)S(1)}, f32[32,2048]{1,0:T(8,128)S(1)}, u32[]{:S(2)}, u32[]{:S(2)}) collective-permute-start(f32[32,2048]{1,0:T(8,128)S(1)} %collective-permute-done.18.refs_5_), channel_id=1, source_target_pairs={{0,4},{4,0},{8,12},{12,8},{16,20},{20,16},{24,28},{28,24},{1,5},{5... | collective-permute-start | bytes 786440 | tf_op jit(solution)/shard_map/ppermute | solution.py:252
  274.0 78.1 %reduce-scatter.6.cloned.1.call-start = ((), (), s32[]{:S(2)}) async-start(), calls=%async_computation.5 | async-start | bytes 1310720 | tf_op jit(solution)/shard_map/reduce_scatter | solution.py:269
  274.1 9.2 %collective-permute-start.3 = (f32[32,2048]{1,0:T(8,128)S(1)}, f32[32,2048]{1,0:T(8,128)S(1)}, u32[]{:S(2)}, u32[]{:S(2)}) collective-permute-start(f32[32,2048]{1,0:T(8,128)S(1)} %copy-done.2), channel_id=1, source_target_pairs={{0,8},{4,12},{8,0},{12,4},{16,24},{20,28},{24,16},{28,20},{1,9},{5... | collective-permute-start | bytes 786440 | tf_op jit(solution)/shard_map/ppermute | solution.py:252
  275.5 9.2 %collective-permute-start.8 = (f32[32,2048]{1,0:T(8,128)S(1)}, f32[32,2048]{1,0:T(8,128)S(1)}, u32[]{:S(2)}, u32[]{:S(2)}) collective-permute-start(f32[32,2048]{1,0:T(8,128)S(1)} %copy-done.3), channel_id=1, source_target_pairs={{0,16},{4,20},{8,24},{12,28},{16,0},{20,4},{24,8},{28,12},{1,17},{... | collective-permute-start | bytes 786440 | tf_op jit(solution)/shard_map/ppermute | solution.py:252
  277.0 11.1 %collective-permute-start.4 = (f32[32,2048]{1,0:T(8,128)S(1)}, f32[32,2048]{1,0:T(8,128)S(1)}, u32[]{:S(2)}, u32[]{:S(2)}) collective-permute-start(f32[32,2048]{1,0:T(8,128)S(1)} %copy-done.3), channel_id=1, source_target_pairs={{0,8},{4,12},{8,0},{12,4},{16,24},{20,28},{24,16},{28,20},{1,9},{5... | collective-permute-start | bytes 786440 | tf_op jit(solution)/shard_map/ppermute | solution.py:252
  277.6 12.8 %collective-permute-start.7 = (f32[32,2048]{1,0:T(8,128)S(1)}, f32[32,2048]{1,0:T(8,128)S(1)}, u32[]{:S(2)}, u32[]{:S(2)}) collective-permute-start(f32[32,2048]{1,0:T(8,128)S(1)} %copy-done.2), channel_id=1, source_target_pairs={{0,16},{4,20},{8,24},{12,28},{16,0},{20,4},{24,8},{28,12},{1,17},{... | collective-permute-start | bytes 786440 | tf_op jit(solution)/shard_map/ppermute | solution.py:252
  278.2 12.2 %collective-permute-start.1 = (f32[32,2048]{1,0:T(8,128)S(1)}, f32[32,2048]{1,0:T(8,128)S(1)}, u32[]{:S(2)}, u32[]{:S(2)}) collective-permute-start(f32[32,2048]{1,0:T(8,128)S(1)} %copy-done.2), channel_id=1, source_target_pairs={{0,4},{4,0},{8,12},{12,8},{16,20},{20,16},{24,28},{28,24},{1,5},{5... | collective-permute-start | bytes 786440 | tf_op jit(solution)/shard_map/ppermute | solution.py:252
  283.3 7.6 %collective-permute-start.2 = (f32[32,2048]{1,0:T(8,128)S(1)}, f32[32,2048]{1,0:T(8,128)S(1)}, u32[]{:S(2)}, u32[]{:S(2)}) collective-permute-start(f32[32,2048]{1,0:T(8,128)S(1)} %copy-done.3), channel_id=1, source_target_pairs={{0,4},{4,0},{8,12},{12,8},{16,20},{20,16},{24,28},{28,24},{1,5},{5... | collective-permute-start | bytes 786440 | tf_op jit(solution)/shard_map/ppermute | solution.py:252
  284.7 10.1 %collective-permute-start.11 = (f32[32,2048]{1,0:T(8,128)S(1)}, f32[32,2048]{1,0:T(8,128)S(1)}, u32[]{:S(2)}, u32[]{:S(2)}) collective-permute-start(f32[32,2048]{1,0:T(8,128)S(1)} %collective-permute-done.3.refs_4_), channel_id=1, source_target_pairs={{0,16},{4,20},{8,24},{12,28},{16,0},{20,4},{24,8},{28,12},{1,17},{... | collective-permute-start | bytes 786440 | tf_op jit(solution)/shard_map/ppermute | solution.py:252
  288.1 7.6 %collective-permute-start.12 = (f32[32,2048]{1,0:T(8,128)S(1)}, f32[32,2048]{1,0:T(8,128)S(1)}, u32[]{:S(2)}, u32[]{:S(2)}) collective-permute-start(f32[32,2048]{1,0:T(8,128)S(1)} %collective-permute-done.8.refs_9_), channel_id=1, source_target_pairs={{0,8},{4,12},{8,0},{12,4},{16,24},{20,28},{24,16},{28,20},{1,9},{5... | collective-permute-start | bytes 786440 | tf_op jit(solution)/shard_map/ppermute | solution.py:252
  290.4 5.4 %collective-permute-start.10 = (f32[32,2048]{1,0:T(8,128)S(1)}, f32[32,2048]{1,0:T(8,128)S(1)}, u32[]{:S(2)}, u32[]{:S(2)}) collective-permute-start(f32[32,2048]{1,0:T(8,128)S(1)} %collective-permute-done.8.refs_9_), channel_id=1, source_target_pairs={{0,4},{4,0},{8,12},{12,8},{16,20},{20,16},{24,28},{28,24},{1,5},{5... | collective-permute-start | bytes 786440 | tf_op jit(solution)/shard_map/ppermute | solution.py:252
  290.4 5.9 %collective-permute-start.5 = (f32[32,2048]{1,0:T(8,128)S(1)}, f32[32,2048]{1,0:T(8,128)S(1)}, u32[]{:S(2)}, u32[]{:S(2)}) collective-permute-start(f32[32,2048]{1,0:T(8,128)S(1)} %collective-permute-done.3.refs_4_), channel_id=1, source_target_pairs={{0,4},{4,0},{8,12},{12,8},{16,20},{20,16},{24,28},{28,24},{1,5},{5... | collective-permute-start | bytes 786440 | tf_op jit(solution)/shard_map/ppermute | solution.py:252
  290.9 5.4 %collective-permute-start.6 = (f32[32,2048]{1,0:T(8,128)S(1)}, f32[32,2048]{1,0:T(8,128)S(1)}, u32[]{:S(2)}, u32[]{:S(2)}) collective-permute-start(f32[32,2048]{1,0:T(8,128)S(1)} %collective-permute-done.4.refs_5_), channel_id=1, source_target_pairs={{0,4},{4,0},{8,12},{12,8},{16,20},{20,16},{24,28},{28,24},{1,5},{5... | collective-permute-start | bytes 786440 | tf_op jit(solution)/shard_map/ppermute | solution.py:252
  (92 other events, 1055.8 us)
Sparse Core Ops, SparseCore 0:
  105.5 28.3 reduce-scatter.13
  162.6 28.2 reduce-scatter.11
  216.6 28.1 reduce-scatter.9
  274.1 28.0 reduce-scatter.7
  324.0 28.0 reduce-scatter.5

commit v3 on v2

--- a/solution.py
+++ b/solution.py
@@ -11,7 +11,7 @@
 VIRT_CAP = 128
 VIRTUALS = 640
 ROW_OCC = 4
-CHUNKS = 5
+ROW_ALIGN = 16
 VMEM_LIMIT = 56 * 1024 * 1024
 
 
@@ -94,24 +94,24 @@
                         out[pl.ds(r, 1), :] = parts[m][g, pl.ds(row, 1), :]
 
 
-def compact_rows(occ_irrep, vir_count, parts):
+def compact_rows(occ_irrep, vir_count, parts, chunks):
     group = len(parts)
-    half = VIRTUALS // (CHUNKS * group * 2)
+    half = VIRTUALS // (chunks * group * 2)
     pairs = parts[0].shape[2]
     vmem = pl.BlockSpec(memory_space=pltpu.VMEM)
     smem = pl.BlockSpec(memory_space=pltpu.SMEM)
     return pl.pallas_call(
         functools.partial(compact_kernel, group),
-        out_shape=[jax.ShapeDtypeStruct((half, pairs), jnp.float32)] * (2 * CHUNKS),
+        out_shape=[jax.ShapeDtypeStruct((half, pairs), jnp.float32)] * (2 * chunks),
         in_specs=[smem, smem] + [vmem] * group,
-        out_specs=[vmem] * (2 * CHUNKS),
+        out_specs=[vmem] * (2 * chunks),
         compiler_params=pltpu.CompilerParams(vmem_limit_bytes=VMEM_LIMIT),
     )(occ_irrep, vir_count, *parts)
 
 
 def product_kernel(group, chunk, irrep_ref, count_ref, *refs):
     n_parts = 2 * group * ROW_OCC
-    parts, (whi_ref, wlo_ref, out_ref, rows_ref, both_ref) = refs[:n_parts], refs[n_parts:]
+    parts, (whi_ref, wlo_ref, out_ref, rows_ref, hi_ref, lo_ref) = refs[:n_parts], refs[n_parts:]
     i, h = pl.program_id(0), pl.program_id(1)
     me = lax.axis_index("pair")
     sub, mine = lax.rem(me, group), lax.div(me, group)
@@ -133,8 +133,8 @@
 
         value = rows_ref[...]
         high = value.astype(jnp.bfloat16)
-        both_ref[:rows, :] = high
-        both_ref[rows:, :] = (value - high.astype(jnp.float32)).astype(jnp.bfloat16)
+        hi_ref[...] = high
+        lo_ref[...] = (value - high.astype(jnp.float32)).astype(jnp.bfloat16)
         out_ref[...] = jnp.zeros_like(out_ref)
 
     offs = offsets_of(count_ref)
@@ -142,15 +142,21 @@
 
     @pl.when((low < rows) & (top > 0))
     def _():
-        first = jnp.dot(both_ref[...], whi_ref[0], preferred_element_type=jnp.float32)
-        second = jnp.dot(both_ref[:rows, :], wlo_ref[0], preferred_element_type=jnp.float32)
-        total = first[:rows] + (first[rows:] + second)
-        row = lax.broadcasted_iota(jnp.int32, total.shape, 0)
-        out_ref[0] = jnp.where((row >= low) & (row < top), total, out_ref[0])
+        window = min(rows, VIRT_CAP + ROW_ALIGN)
+        base = lax.div(jnp.maximum(low, 0), ROW_ALIGN) * ROW_ALIGN
+        base = pl.multiple_of(jnp.minimum(base, rows - window), ROW_ALIGN)
+        high, rest = hi_ref[pl.ds(base, window), :], lo_ref[pl.ds(base, window), :]
+        both = jnp.concatenate([high, rest], axis=0)
+        first = jnp.dot(both, whi_ref[0], preferred_element_type=jnp.float32)
+        second = jnp.dot(high, wlo_ref[0], preferred_element_type=jnp.float32)
+        total = first[:window] + (first[window:] + second)
+        row = base + lax.broadcasted_iota(jnp.int32, total.shape, 0)
+        spot = pl.ds(base, window)
+        out_ref[0, spot, :] = jnp.where((row >= low) & (row < top), total, out_ref[0, spot, :])
 
 
 def product(occ_irrep, vir_count, chunk, parts, w_hi, w_lo, group):
-    rows = VIRTUALS // CHUNKS
+    rows = 2 * group * parts[0].shape[0]
     irreps, pairs, cols = w_hi.shape
 
     def block_of(i, h, irrep_ref, count_ref):
@@ -171,7 +177,7 @@
             grid=(ROW_OCC, irreps),
             in_specs=[t_spec] * len(parts) + [w_spec, w_spec],
             out_specs=pl.BlockSpec((1, rows, cols), lambda i, h, *_: (i, 0, 0)),
-            scratch_shapes=[pltpu.VMEM((rows, pairs), jnp.float32), pltpu.VMEM((2 * rows, pairs), jnp.bfloat16)],
+            scratch_shapes=[pltpu.VMEM((rows, pairs), dtype) for dtype in (jnp.float32, jnp.bfloat16, jnp.bfloat16)],
         ),
         compiler_params=pltpu.CompilerParams(vmem_limit_bytes=VMEM_LIMIT),
         cost_estimate=pl.CostEstimate(
@@ -182,7 +188,7 @@
 
 
 def expand_kernel(share, irrep_ref, count_ref, occ_ref, vir_ref, vir_t_ref, *refs):
-    pieces, (out_ref, all_ref) = refs[:CHUNKS], refs[CHUNKS:]
+    pieces, (out_ref, all_ref) = refs[:-2], refs[-2:]
     g = pl.program_id(0)
     ph, pair = lax.axis_index("ph"), lax.axis_index("pair")
     rows = pieces[0].shape[0]
@@ -192,11 +198,11 @@
     def _():
         for s, piece in enumerate(pieces):
             all_ref[s * rows : (s + 1) * rows, :] = piece[...]
-        all_ref[CHUNKS * rows :, :] = jnp.zeros_like(all_ref[CHUNKS * rows :, :])
+        all_ref[VIRTUALS:, :] = jnp.zeros_like(all_ref[VIRTUALS:, :])
 
     i, first_slot = lax.div(ph, share), lax.rem(ph, share) * out_rows
     h = jnp.bitwise_xor(irrep_ref[i], g)
-    start = jnp.minimum(pick(offsets_of(count_ref)[:-1], h) + first_slot, CHUNKS * rows)
+    start = jnp.minimum(pick(offsets_of(count_ref)[:-1], h) + first_slot, VIRTUALS)
     base = pl.multiple_of(lax.div(start, 8) * 8, 8)
     window = all_ref[pl.ds(base, out_rows + 8), :]
     window = pltpu.roll(window, lax.rem(out_rows + 8 - (start - base), out_rows + 8), 0)[:out_rows]
@@ -223,7 +229,6 @@
 
 def expand(occ_irrep, vir_count, occ_energy, vir_energy, pieces, out_rows, share):
     cols = pieces[0].shape[1]
-    rows = VIRTUALS // CHUNKS
     smem = pl.BlockSpec(memory_space=pltpu.SMEM)
 
     def whole(array):
@@ -236,7 +241,7 @@
         grid=(IRREPS,),
         in_specs=[smem, smem, smem, whole(vir_energy), whole(vir_t)] + [whole(piece) for piece in pieces],
         out_specs=pl.BlockSpec((1, out_rows, cols), lambda g: (g, 0, 0)),
-        scratch_shapes=[pltpu.VMEM((CHUNKS * rows + out_rows + 8, cols), jnp.float32)],
+        scratch_shapes=[pltpu.VMEM((VIRTUALS + out_rows + 8, cols), jnp.float32)],
         compiler_params=pltpu.CompilerParams(vmem_limit_bytes=VMEM_LIMIT),
     )(occ_irrep, vir_count, occ_energy, vir_energy, vir_t, *pieces)
 
@@ -252,10 +257,11 @@
         return lax.ppermute(array, "pair", [(d, d ^ bits) for d in range(n_pair)])
 
     parts = [t_cycle] + [swap(t_cycle, m) for m in range(1, group)]
-    own = compact_rows(occ_irrep, vir_count, parts)
+    chunks = next(n for n in (2, 5, 1) if VIRTUALS % (16 * n * group) == 0)
+    own = compact_rows(occ_irrep, vir_count, parts, chunks)
     w_hi, w_lo = split_weights(occ_irrep, vir_count, w_cycle)
     pieces = []
-    for s in range(CHUNKS):
+    for s in range(chunks):
         a, b = own[2 * s], own[2 * s + 1]
         near_a, near_b = swap(a, group), swap(b, group)
         far_a, far_b = swap(a, 2 * group), swap(b, 2 * group)

time: 364 us -> 313 us (0.86)
  Pallas kernels: 189 us -> 136 us
  waiting for transfers between devices: 110 us -> 140 us
  starting transfers between devices: 42.6 us -> 18 us
    pallas_call x5 -> x2, Pallas kernels: 144 us -> 91 us  [product(): pl.pallas_call(functools.partial(product_kernel, group, chunk), out_shape...]
    ppermute x71 -> x29, starting transfers between devices: 42.3 us -> 17.9 us  [swap(): return lax.ppermute(array, 'pair', [(d, d ^ bits) for d in range(n_pair)])]
    reduce_scatter x5 -> x2, waiting for transfers between devices: 27.5 us -> 51.8 us  [on_device(): lax.psum_scatter(partial_value, 'ph', scatter_dimension=0, tiled=True)]
    ppermute x71 -> x29, waiting for transfers between devices: 82.6 us -> 88.4 us  [swap(): return lax.ppermute(array, 'pair', [(d, d ^ bits) for d in range(n_pair)])]
    unnamed x161 -> x59, local copies, waits for them, and re-layouts: 7.77 us -> 4.9 us
  transfers between devices with their start and end apart: 76 -> 31, of which waited for: 44 -> 16; matrix products, arithmetic and copies ran while one was open for 0% -> 0% of each run, Pallas kernels for 41% -> 25%
where the time goes in v3:
time: 313 us
  waiting for transfers between devices  140 us (45%)
  Pallas kernels  136 us (43%)
  starting transfers between devices  18 us (6%)
  between operations  13.7 us (4%)
  local copies, waits for them, and re-layouts  4.9 us (2%)
    pallas_call x2, Pallas kernels, product(): pl.pallas_call(functools.partial(product_kernel, group, chunk), out_shape...  91 us
    ppermute x29, waiting for transfers between devices, swap(): return lax.ppermute(array, 'pair', [(d, d ^ bits) for d in range(n_pair)])  88.4 us
    reduce_scatter x2, waiting for transfers between devices, on_device(): lax.psum_scatter(partial_value, 'ph', scatter_dimension=0, tiled=True)  51.8 us
    pallas_call x1, Pallas kernels, split_weights(): pl.pallas_call(split_kernel, out_shape=(part, part), grid_spec=pltpu.Pref...  29.3 us
    ppermute x29, starting transfers between devices, swap(): return lax.ppermute(array, 'pair', [(d, d ^ bits) for d in range(n_pair)])  17.9 us
    pallas_call x1, Pallas kernels, compact_rows(): pl.pallas_call(functools.partial(compact_kernel, group), out_shape=[jax.S...  10.9 us
  transfers between devices with their start and end apart: 31, of which 16 were waited for; matrix products, arithmetic and copies ran while one was open for 0% of the time, Pallas kernels for 25%

profile of v3, /device:TPU:0, one launch (start us, length us, event | category | flops | bytes accessed | tf_op | source)
XLA Modules:
  0.0 313.3 jit_solution(12600283261637403808)
XLA Ops:
  6.5 0.5 collective-permute-start
  7.0 7.0 %collective-permute-done.refs_1_ = f32[8,64,2048]{2,1,0:T(8,128)S(1)} collective-permute-done((f32[8,64,2048]{2,1,0:T(8,128)}, f32[8,64,2048]{2,1,0:T(8,128)S(1)}, u32[]{:S(2)}, u32[]{:S(2)}) %collective-permute-start) | collective-permute-done | bytes 4194336 | tf_op jit(solution)/shard_map/ppermute | solution.py:257
  14.0 2.0 copy-done
  16.0 10.9 %shard_map.64 = (f32[80,2048]{1,0:T(8,128)}, f32[80,2048]{1,0:T(8,128)}, f32[80,2048]{1,0:T(8,128)}, f32[80,2048]{1,0:T(8,128)}) custom-call(s32[64]{0:T(128)} %irrep_ref.9, s32[8]{0:T(128)} %count_ref.9, f32[8,64,2048]{2,1,0:T(8,128)} %refs_0_.1, f32[8,64,2048]{2,1,0:T(8,128)} %copy-done), custom_call_target="tpu_custom_call" | custom-call | tf_op jit(solution)/shard_map/pallas_call | solution.py:103
  26.9 2.9 collective-permute-start.17
  29.8 1.6 collective-permute-start.22
  31.3 0.5 collective-permute-start.18
  31.8 0.0 collective-permute-start.21
  31.8 0.0 collective-permute-start.15
  31.8 13.7 %collective-permute-done.17.refs_4_ = f32[80,2048]{1,0:T(8,128)S(1)} collective-permute-done((f32[80,2048]{1,0:T(8,128)}, f32[80,2048]{1,0:T(8,128)S(1)}, u32[]{:S(2)}, u32[]{:S(2)}) %collective-permute-start.17) | collective-permute-done | bytes 655392 | tf_op jit(solution)/shard_map/ppermute | solution.py:257
  45.5 0.0 collective-permute-start.16
  45.5 2.1 collective-permute-done.22.refs_9_
  47.6 1.6 collective-permute-start.25
  49.1 9.9 %collective-permute-done.18.refs_5_ = f32[80,2048]{1,0:T(8,128)S(1)} collective-permute-done((f32[80,2048]{1,0:T(8,128)}, f32[80,2048]{1,0:T(8,128)S(1)}, u32[]{:S(2)}, u32[]{:S(2)}) %collective-permute-start.18) | collective-permute-done | bytes 655392 | tf_op jit(solution)/shard_map/ppermute | solution.py:257
  59.0 1.7 collective-permute-start.26
  60.8 0.8 collective-permute-done.21.refs_8_
  61.6 0.5 collective-permute-start.24
  62.1 0.1 collective-permute-start.20
  62.2 12.3 %collective-permute-done.25.refs_12_ = f32[80,2048]{1,0:T(8,128)S(1)} collective-permute-done((f32[80,2048]{1,0:T(8,128)S(1)}, f32[80,2048]{1,0:T(8,128)S(1)}, u32[]{:S(2)}, u32[]{:S(2)}) %collective-permute-start.25) | collective-permute-done | bytes 655392 | tf_op jit(solution)/shard_map/ppermute | solution.py:257
  74.5 0.8 collective-permute-done.26.refs_13_
  75.3 0.0 collective-permute-start.27
  75.3 0.0 collective-permute-done.19.refs_6_
  75.3 0.5 collective-permute-start.28
  75.8 29.3 %shard_map.65 = (bf16[8,2048,512]{2,1,0:T(8,128)(2,1)}, bf16[8,2048,512]{2,1,0:T(8,128)(2,1)}) custom-call(s32[64]{0:T(128)} %irrep_ref.9, s32[8]{0:T(128)} %count_ref.9, f32[8,2048,512]{2,1,0:T(8,128)} %w_ref.1), custom_call_target="tpu_custom_call" | custom-call | flops 33554432 | bytes 67108864 | tf_op jit(solution)/shard_map/pallas_call | solution.py:52
  105.2 0.0 collective-permute-done.24.refs_11_
  105.3 0.0 collective-permute-done.20.refs_7_
  105.3 0.0 collective-permute-done.27.refs_14_
  105.3 0.0 collective-permute-done.28.refs_15_
  105.3 0.9 copy-done.24
  106.2 0.2 copy-done.26
  106.4 0.2 copy-done.22
  106.6 40.6 %shard_map.67 = f32[4,320,512]{2,1,0:T(8,128)} custom-call(s32[64]{0:T(128)} %irrep_ref.9, s32[8]{0:T(128)} %count_ref.9, f32[80,2048]{1,0:T(8,128)} %get-tuple-element.15.refs_0_, f32[80,2048]{1,0:T(8,128)} %get-tuple-element.16.refs_1_, f32[80,2048]{1,0:T(8,128)} %copy-done.12, f32[80,2048]{1,0:T(8,128)} %copy-done.14, f32[80,2048]{1,0:T(8,128)} %copy-done.4, ...), custom_call_target="tpu_custom_call" | custom-call | flops 32212254720 | bytes 41943040 | tf_op jit(solution)/shard_map/pallas_call | solution.py:172
  147.1 0.0 reduce-scatter.5.cloned.1.call-update
  147.1 0.0 reduce-scatter.3.cloned.1.call-start
  147.2 1.5 collective-permute-start.3
  148.7 1.5 collective-permute-start.8
  150.2 0.5 collective-permute-start.4
  150.8 0.6 collective-permute-start.7
  151.3 0.0 collective-permute-start.1
  151.3 13.5 %collective-permute-done.3.refs_4_ = f32[80,2048]{1,0:T(8,128)S(1)} collective-permute-done((f32[80,2048]{1,0:T(8,128)S(1)}, f32[80,2048]{1,0:T(8,128)S(1)}, u32[]{:S(2)}, u32[]{:S(2)}) %collective-permute-start.3) | collective-permute-done | bytes 655392 | tf_op jit(solution)/shard_map/ppermute | solution.py:257
  164.9 0.0 collective-permute-start.2
  164.9 1.5 collective-permute-done.8.refs_9_
  166.3 1.5 collective-permute-start.11
  167.8 10.2 %collective-permute-done.4.refs_5_ = f32[80,2048]{1,0:T(8,128)S(1)} collective-permute-done((f32[80,2048]{1,0:T(8,128)S(1)}, f32[80,2048]{1,0:T(8,128)S(1)}, u32[]{:S(2)}, u32[]{:S(2)}) %collective-permute-start.4) | collective-permute-done | bytes 655392 | tf_op jit(solution)/shard_map/ppermute | solution.py:257
  178.0 1.4 collective-permute-start.12
  179.5 0.9 collective-permute-done.7.refs_8_
  180.4 0.5 collective-permute-start.5
  180.9 0.0 collective-permute-done.2.refs_3_
  180.9 0.1 collective-permute-start.6
  181.0 12.2 %collective-permute-done.11.refs_12_ = f32[80,2048]{1,0:T(8,128)S(1)} collective-permute-done((f32[80,2048]{1,0:T(8,128)S(1)}, f32[80,2048]{1,0:T(8,128)S(1)}, u32[]{:S(2)}, u32[]{:S(2)}) %collective-permute-start.11) | collective-permute-done | bytes 655392 | tf_op jit(solution)/shard_map/ppermute | solution.py:257
  193.2 0.0 collective-permute-start.9
  193.2 0.8 collective-permute-done.12.refs_13_
  194.0 0.0 collective-permute-done.10.refs_11_
  194.0 0.5 collective-permute-start.14
  194.5 0.0 collective-permute-done.5.refs_6_
  194.5 0.0 collective-permute-done.6.refs_7_
  194.6 0.8 collective-permute-done.9.refs_10_
  195.3 1.9 collective-permute-done.13.refs_14_
  197.2 0.8 copy-done.28
  198.2 50.5 %shard_map.66 = f32[4,320,512]{2,1,0:T(8,128)} custom-call(s32[64]{0:T(128)} %irrep_ref.9, s32[8]{0:T(128)} %count_ref.9, f32[80,2048]{1,0:T(8,128)} %get-tuple-element.11.refs_0_, f32[80,2048]{1,0:T(8,128)} %get-tuple-element.12.refs_1_, f32[80,2048]{1,0:T(8,128)} %copy-done.13, f32[80,2048]{1,0:T(8,128)} %copy-done.15, f32[80,2048]{1,0:T(8,128)} %copy-done.5, ...), custom_call_target="tpu_custom_call" | custom-call | flops 32212254720 | bytes 41943040 | tf_op jit(solution)/shard_map/pallas_call | solution.py:172
  248.6 0.0 reduce-scatter.3.cloned.1.call-update
  248.7 0.7 copy.7
  249.4 51.8 %reduce-scatter.3.cloned.1.call-done.refs_0_ = f32[320,512]{1,0:T(8,128)} async-done(((f32[1280,512]{1,0:T(8,128)}), f32[320,512]{1,0:T(8,128)}) %reduce-scatter.3.cloned.1.call-update) | async-done | bytes 655376 | tf_op jit(solution)/shard_map/reduce_scatter | solution.py:275
  301.2 5.2 %shard_map.68 = f32[8,128,512]{2,1,0:T(8,128)} custom-call(s32[64]{0:T(128)} %irrep_ref.9, s32[8]{0:T(128)} %count_ref.9, f32[64]{0:T(128)} %occ_ref.1, f32[8,128]{1,0:T(8,128)} %vir_ref.1, f32[128,8]{1,0:T(8,128)} %bitcast.5, f32[320,512]{1,0:T(8,128)} %reduce-scatter.3.cloned.1.call-done.refs_0_, f32[320,512]{1,0:T(8,128)} %reduce-scatter.5.cloned.1.call-done.refs_1_), custom_call_target="tpu_custom_call" | custom-call | tf_op jit(solution)/shard_map/pallas_call | solution.py:238
  (64 shorter events, 0.1 us)
Async XLA Ops:
  6.5 242.9 %reduce-scatter.5.cloned.1.call-start = ((), (), s32[]{:S(2)}) async-start(), calls=%async_computation.3 | async-start | bytes 3276800 | tf_op jit(solution)/shard_map/reduce_scatter | solution.py:275
  6.5 7.4 %collective-permute-start = (f32[8,64,2048]{2,1,0:T(8,128)}, f32[8,64,2048]{2,1,0:T(8,128)S(1)}, u32[]{:S(2)}, u32[]{:S(2)}) collective-permute-start(f32[8,64,2048]{2,1,0:T(8,128)} %refs_0_.1), channel_id=1, source_target_pairs={{0,4},{4,0},{8,12},{12,8},{16,20},{20,16},{24,28},{28,24},{1,5},{5... | collective-permute-start | bytes 12582920 | tf_op jit(solution)/shard_map/ppermute | solution.py:257
  14.0 2.0 copy-start
  26.9 18.6 %collective-permute-start.17 = (f32[80,2048]{1,0:T(8,128)}, f32[80,2048]{1,0:T(8,128)S(1)}, u32[]{:S(2)}, u32[]{:S(2)}) collective-permute-start(f32[80,2048]{1,0:T(8,128)} %get-tuple-element.15.refs_0_), channel_id=1, source_target_pairs={{0,8},{4,12},{8,0},{12,4},{16,24},{20,28},{24,16},{28,20},{1,9},{5... | collective-permute-start | bytes 1966088 | tf_op jit(solution)/shard_map/ppermute | solution.py:257
  29.8 17.8 %collective-permute-start.22 = (f32[80,2048]{1,0:T(8,128)}, f32[80,2048]{1,0:T(8,128)S(1)}, u32[]{:S(2)}, u32[]{:S(2)}) collective-permute-start(f32[80,2048]{1,0:T(8,128)} %get-tuple-element.16.refs_1_), channel_id=1, source_target_pairs={{0,16},{4,20},{8,24},{12,28},{16,0},{20,4},{24,8},{28,12},{1,17},{... | collective-permute-start | bytes 1966088 | tf_op jit(solution)/shard_map/ppermute | solution.py:257
  31.3 27.7 %collective-permute-start.18 = (f32[80,2048]{1,0:T(8,128)}, f32[80,2048]{1,0:T(8,128)S(1)}, u32[]{:S(2)}, u32[]{:S(2)}) collective-permute-start(f32[80,2048]{1,0:T(8,128)} %get-tuple-element.16.refs_1_), channel_id=1, source_target_pairs={{0,8},{4,12},{8,0},{12,4},{16,24},{20,28},{24,16},{28,20},{1,9},{5... | collective-permute-start | bytes 1966088 | tf_op jit(solution)/shard_map/ppermute | solution.py:257
  31.8 29.8 %collective-permute-start.21 = (f32[80,2048]{1,0:T(8,128)}, f32[80,2048]{1,0:T(8,128)S(1)}, u32[]{:S(2)}, u32[]{:S(2)}) collective-permute-start(f32[80,2048]{1,0:T(8,128)} %get-tuple-element.15.refs_0_), channel_id=1, source_target_pairs={{0,16},{4,20},{8,24},{12,28},{16,0},{20,4},{24,8},{28,12},{1,17},{... | collective-permute-start | bytes 1966088 | tf_op jit(solution)/shard_map/ppermute | solution.py:257
  31.8 29.8 %collective-permute-start.15 = (f32[80,2048]{1,0:T(8,128)}, f32[80,2048]{1,0:T(8,128)S(1)}, u32[]{:S(2)}, u32[]{:S(2)}) collective-permute-start(f32[80,2048]{1,0:T(8,128)} %get-tuple-element.15.refs_0_), channel_id=1, source_target_pairs={{0,4},{4,0},{8,12},{12,8},{16,20},{20,16},{24,28},{28,24},{1,5},{5... | collective-permute-start | bytes 1966088 | tf_op jit(solution)/shard_map/ppermute | solution.py:257
  45.5 59.7 %copy-start.4 = (f32[80,2048]{1,0:T(8,128)}, f32[80,2048]{1,0:T(8,128)S(1)}, u32[]{:S(2)}) copy-start(f32[80,2048]{1,0:T(8,128)S(1)} %collective-permute-done.17.refs_4_) | copy-start | bytes 1966084
  45.5 16.7 %collective-permute-start.16 = (f32[80,2048]{1,0:T(8,128)}, f32[80,2048]{1,0:T(8,128)S(1)}, u32[]{:S(2)}, u32[]{:S(2)}) collective-permute-start(f32[80,2048]{1,0:T(8,128)} %get-tuple-element.16.refs_1_), channel_id=1, source_target_pairs={{0,4},{4,0},{8,12},{12,8},{16,20},{20,16},{24,28},{28,24},{1,5},{5... | collective-permute-start | bytes 1966088 | tf_op jit(solution)/shard_map/ppermute | solution.py:257
  47.6 57.6 %copy-start.6 = (f32[80,2048]{1,0:T(8,128)}, f32[80,2048]{1,0:T(8,128)S(1)}, u32[]{:S(2)}) copy-start(f32[80,2048]{1,0:T(8,128)S(1)} %collective-permute-done.22.refs_9_) | copy-start | bytes 1966084
  47.6 27.0 %collective-permute-start.25 = (f32[80,2048]{1,0:T(8,128)S(1)}, f32[80,2048]{1,0:T(8,128)S(1)}, u32[]{:S(2)}, u32[]{:S(2)}) collective-permute-start(f32[80,2048]{1,0:T(8,128)S(1)} %collective-permute-done.17.refs_4_), channel_id=1, source_target_pairs={{0,16},{4,20},{8,24},{12,28},{16,0},{20,4},{24,8},{28,12},{1,17},{... | collective-permute-start | bytes 1966088 | tf_op jit(solution)/shard_map/ppermute | solution.py:257
  59.0 46.1 %copy-start.8 = (f32[80,2048]{1,0:T(8,128)}, f32[80,2048]{1,0:T(8,128)S(1)}, u32[]{:S(2)}) copy-start(f32[80,2048]{1,0:T(8,128)S(1)} %collective-permute-done.18.refs_5_) | copy-start | bytes 1966084
  59.0 16.3 %collective-permute-start.26 = (f32[80,2048]{1,0:T(8,128)S(1)}, f32[80,2048]{1,0:T(8,128)S(1)}, u32[]{:S(2)}, u32[]{:S(2)}) collective-permute-start(f32[80,2048]{1,0:T(8,128)S(1)} %collective-permute-done.22.refs_9_), channel_id=1, source_target_pairs={{0,8},{4,12},{8,0},{12,4},{16,24},{20,28},{24,16},{28,20},{1,9},{5... | collective-permute-start | bytes 1966088 | tf_op jit(solution)/shard_map/ppermute | solution.py:257
  61.6 43.6 %copy-start.10 = (f32[80,2048]{1,0:T(8,128)}, f32[80,2048]{1,0:T(8,128)S(1)}, u32[]{:S(2)}) copy-start(f32[80,2048]{1,0:T(8,128)S(1)} %collective-permute-done.21.refs_8_) | copy-start | bytes 1966084
  61.6 13.7 %collective-permute-start.19 = (f32[80,2048]{1,0:T(8,128)S(1)}, f32[80,2048]{1,0:T(8,128)S(1)}, u32[]{:S(2)}, u32[]{:S(2)}) collective-permute-start(f32[80,2048]{1,0:T(8,128)S(1)} %collective-permute-done.17.refs_4_), channel_id=1, source_target_pairs={{0,4},{4,0},{8,12},{12,8},{16,20},{20,16},{24,28},{28,24},{1,5},{5... | collective-permute-start | bytes 1966088 | tf_op jit(solution)/shard_map/ppermute | solution.py:257
  61.6 43.6 %copy-start.12 = (f32[80,2048]{1,0:T(8,128)}, f32[80,2048]{1,0:T(8,128)S(1)}, u32[]{:S(2)}) copy-start(f32[80,2048]{1,0:T(8,128)S(1)} %collective-permute-done.15.refs_2_) | copy-start | bytes 1966084
  61.6 43.6 %collective-permute-start.24 = (f32[80,2048]{1,0:T(8,128)S(1)}, f32[80,2048]{1,0:T(8,128)S(1)}, u32[]{:S(2)}, u32[]{:S(2)}) collective-permute-start(f32[80,2048]{1,0:T(8,128)S(1)} %collective-permute-done.22.refs_9_), channel_id=1, source_target_pairs={{0,4},{4,0},{8,12},{12,8},{16,20},{20,16},{24,28},{28,24},{1,5},{5... | collective-permute-start | bytes 1966088 | tf_op jit(solution)/shard_map/ppermute | solution.py:257
  62.1 43.1 %copy-start.14 = (f32[80,2048]{1,0:T(8,128)}, f32[80,2048]{1,0:T(8,128)S(1)}, u32[]{:S(2)}) copy-start(f32[80,2048]{1,0:T(8,128)S(1)} %collective-permute-done.16.refs_3_) | copy-start | bytes 1966084
  62.1 43.1 %collective-permute-start.20 = (f32[80,2048]{1,0:T(8,128)S(1)}, f32[80,2048]{1,0:T(8,128)S(1)}, u32[]{:S(2)}, u32[]{:S(2)}) collective-permute-start(f32[80,2048]{1,0:T(8,128)S(1)} %collective-permute-done.18.refs_5_), channel_id=1, source_target_pairs={{0,4},{4,0},{8,12},{12,8},{16,20},{20,16},{24,28},{28,24},{1,5},{5... | collective-permute-start | bytes 1966088 | tf_op jit(solution)/shard_map/ppermute | solution.py:257
  74.5 30.7 %copy-start.16 = (f32[80,2048]{1,0:T(8,128)}, f32[80,2048]{1,0:T(8,128)S(1)}, u32[]{:S(2)}) copy-start(f32[80,2048]{1,0:T(8,128)S(1)} %collective-permute-done.25.refs_12_) | copy-start | bytes 1966084
  74.5 30.7 %collective-permute-start.23 = (f32[80,2048]{1,0:T(8,128)S(1)}, f32[80,2048]{1,0:T(8,128)S(1)}, u32[]{:S(2)}, u32[]{:S(2)}) collective-permute-start(f32[80,2048]{1,0:T(8,128)S(1)} %collective-permute-done.21.refs_8_), channel_id=1, source_target_pairs={{0,4},{4,0},{8,12},{12,8},{16,20},{20,16},{24,28},{28,24},{1,5},{5... | collective-permute-start | bytes 1966088 | tf_op jit(solution)/shard_map/ppermute | solution.py:257
  75.3 29.9 %copy-start.18 = (f32[80,2048]{1,0:T(8,128)}, f32[80,2048]{1,0:T(8,128)S(1)}, u32[]{:S(2)}) copy-start(f32[80,2048]{1,0:T(8,128)S(1)} %collective-permute-done.26.refs_13_) | copy-start | bytes 1966084
  75.3 30.0 %collective-permute-start.27 = (f32[80,2048]{1,0:T(8,128)S(1)}, f32[80,2048]{1,0:T(8,128)}, u32[]{:S(2)}, u32[]{:S(2)}) collective-permute-start(f32[80,2048]{1,0:T(8,128)S(1)} %collective-permute-done.25.refs_12_), channel_id=1, source_target_pairs={{0,4},{4,0},{8,12},{12,8},{16,20},{20,16},{24,28},{28,24},{1,5},{5... | collective-permute-start | bytes 1966088 | tf_op jit(solution)/shard_map/ppermute | solution.py:257
  75.3 29.9 %copy-start.20 = (f32[80,2048]{1,0:T(8,128)}, f32[80,2048]{1,0:T(8,128)S(1)}, u32[]{:S(2)}) copy-start(f32[80,2048]{1,0:T(8,128)S(1)} %collective-permute-done.19.refs_6_) | copy-start | bytes 1966084
  75.3 30.0 %collective-permute-start.28 = (f32[80,2048]{1,0:T(8,128)S(1)}, f32[80,2048]{1,0:T(8,128)}, u32[]{:S(2)}, u32[]{:S(2)}) collective-permute-start(f32[80,2048]{1,0:T(8,128)S(1)} %collective-permute-done.26.refs_13_), channel_id=1, source_target_pairs={{0,4},{4,0},{8,12},{12,8},{16,20},{20,16},{24,28},{28,24},{1,5},{5... | collective-permute-start | bytes 1966088 | tf_op jit(solution)/shard_map/ppermute | solution.py:257
  105.3 1.3 copy-start.22
  105.3 0.9 copy-start.24
  105.3 1.1 copy-start.26
  106.6 40.6 %copy-start.2 = (f32[80,2048]{1,0:T(8,128)S(1)}, f32[80,2048]{1,0:T(8,128)}, u32[]{:S(2)}) copy-start(f32[80,2048]{1,0:T(8,128)} %get-tuple-element.11.refs_0_) | copy-start | bytes 1966084
  106.6 42.1 %copy-start.3 = (f32[80,2048]{1,0:T(8,128)S(1)}, f32[80,2048]{1,0:T(8,128)}, u32[]{:S(2)}) copy-start(f32[80,2048]{1,0:T(8,128)} %get-tuple-element.12.refs_1_) | copy-start | bytes 1966084
  147.1 154.1 %reduce-scatter.3.cloned.1.call-start = ((), (), s32[]{:S(2)}) async-start(), calls=%async_computation.2 | async-start | bytes 3276800 | tf_op jit(solution)/shard_map/reduce_scatter | solution.py:275
  147.2 17.7 %collective-permute-start.3 = (f32[80,2048]{1,0:T(8,128)S(1)}, f32[80,2048]{1,0:T(8,128)S(1)}, u32[]{:S(2)}, u32[]{:S(2)}) collective-permute-start(f32[80,2048]{1,0:T(8,128)S(1)} %copy-done.2), channel_id=1, source_target_pairs={{0,8},{4,12},{8,0},{12,4},{16,24},{20,28},{24,16},{28,20},{1,9},{5... | collective-permute-start | bytes 1966088 | tf_op jit(solution)/shard_map/ppermute | solution.py:257
  148.7 100.0 %copy-start.1 = (f32[8,128]{1,0:T(8,128)S(1)}, f32[8,128]{1,0:T(8,128)}, u32[]{:S(2)}) copy-start(f32[8,128]{1,0:T(8,128)} %vir_ref.1) | copy-start | bytes 12292
  148.7 17.6 %collective-permute-start.8 = (f32[80,2048]{1,0:T(8,128)S(1)}, f32[80,2048]{1,0:T(8,128)S(1)}, u32[]{:S(2)}, u32[]{:S(2)}) collective-permute-start(f32[80,2048]{1,0:T(8,128)S(1)} %copy-done.3), channel_id=1, source_target_pairs={{0,16},{4,20},{8,24},{12,28},{16,0},{20,4},{24,8},{28,12},{1,17},{... | collective-permute-start | bytes 1966088 | tf_op jit(solution)/shard_map/ppermute | solution.py:257
  150.2 27.8 %collective-permute-start.4 = (f32[80,2048]{1,0:T(8,128)S(1)}, f32[80,2048]{1,0:T(8,128)S(1)}, u32[]{:S(2)}, u32[]{:S(2)}) collective-permute-start(f32[80,2048]{1,0:T(8,128)S(1)} %copy-done.3), channel_id=1, source_target_pairs={{0,8},{4,12},{8,0},{12,4},{16,24},{20,28},{24,16},{28,20},{1,9},{5... | collective-permute-start | bytes 1966088 | tf_op jit(solution)/shard_map/ppermute | solution.py:257
  150.8 29.6 %collective-permute-start.7 = (f32[80,2048]{1,0:T(8,128)S(1)}, f32[80,2048]{1,0:T(8,128)S(1)}, u32[]{:S(2)}, u32[]{:S(2)}) collective-permute-start(f32[80,2048]{1,0:T(8,128)S(1)} %copy-done.2), channel_id=1, source_target_pairs={{0,16},{4,20},{8,24},{12,28},{16,0},{20,4},{24,8},{28,12},{1,17},{... | collective-permute-start | bytes 1966088 | tf_op jit(solution)/shard_map/ppermute | solution.py:257
  151.3 29.1 %collective-permute-start.1 = (f32[80,2048]{1,0:T(8,128)S(1)}, f32[80,2048]{1,0:T(8,128)S(1)}, u32[]{:S(2)}, u32[]{:S(2)}) collective-permute-start(f32[80,2048]{1,0:T(8,128)S(1)} %copy-done.2), channel_id=1, source_target_pairs={{0,4},{4,0},{8,12},{12,8},{16,20},{20,16},{24,28},{28,24},{1,5},{5... | collective-permute-start | bytes 1966088 | tf_op jit(solution)/shard_map/ppermute | solution.py:257
  164.9 33.2 %copy-start.5 = (f32[80,2048]{1,0:T(8,128)}, f32[80,2048]{1,0:T(8,128)S(1)}, u32[]{:S(2)}) copy-start(f32[80,2048]{1,0:T(8,128)S(1)} %collective-permute-done.3.refs_4_) | copy-start | bytes 1966084
  164.9 16.0 %collective-permute-start.2 = (f32[80,2048]{1,0:T(8,128)S(1)}, f32[80,2048]{1,0:T(8,128)S(1)}, u32[]{:S(2)}, u32[]{:S(2)}) collective-permute-start(f32[80,2048]{1,0:T(8,128)S(1)} %copy-done.3), channel_id=1, source_target_pairs={{0,4},{4,0},{8,12},{12,8},{16,20},{20,16},{24,28},{28,24},{1,5},{5... | collective-permute-start | bytes 1966088 | tf_op jit(solution)/shard_map/ppermute | solution.py:257
  166.3 31.7 %copy-start.7 = (f32[80,2048]{1,0:T(8,128)}, f32[80,2048]{1,0:T(8,128)S(1)}, u32[]{:S(2)}) copy-start(f32[80,2048]{1,0:T(8,128)S(1)} %collective-permute-done.8.refs_9_) | copy-start | bytes 1966084
  166.3 26.9 %collective-permute-start.11 = (f32[80,2048]{1,0:T(8,128)S(1)}, f32[80,2048]{1,0:T(8,128)S(1)}, u32[]{:S(2)}, u32[]{:S(2)}) collective-permute-start(f32[80,2048]{1,0:T(8,128)S(1)} %collective-permute-done.3.refs_4_), channel_id=1, source_target_pairs={{0,16},{4,20},{8,24},{12,28},{16,0},{20,4},{24,8},{28,12},{1,17},{... | collective-permute-start | bytes 1966088 | tf_op jit(solution)/shard_map/ppermute | solution.py:257
  178.0 20.0 %copy-start.9 = (f32[80,2048]{1,0:T(8,128)}, f32[80,2048]{1,0:T(8,128)S(1)}, u32[]{:S(2)}) copy-start(f32[80,2048]{1,0:T(8,128)S(1)} %collective-permute-done.4.refs_5_) | copy-start | bytes 1966084
  178.0 16.0 %collective-permute-start.12 = (f32[80,2048]{1,0:T(8,128)S(1)}, f32[80,2048]{1,0:T(8,128)S(1)}, u32[]{:S(2)}, u32[]{:S(2)}) collective-permute-start(f32[80,2048]{1,0:T(8,128)S(1)} %collective-permute-done.8.refs_9_), channel_id=1, source_target_pairs={{0,8},{4,12},{8,0},{12,4},{16,24},{20,28},{24,16},{28,20},{1,9},{5... | collective-permute-start | bytes 1966088 | tf_op jit(solution)/shard_map/ppermute | solution.py:257
  180.4 17.7 %copy-start.11 = (f32[80,2048]{1,0:T(8,128)}, f32[80,2048]{1,0:T(8,128)S(1)}, u32[]{:S(2)}) copy-start(f32[80,2048]{1,0:T(8,128)S(1)} %collective-permute-done.7.refs_8_) | copy-start | bytes 1966084
  180.4 13.7 %collective-permute-start.10 = (f32[80,2048]{1,0:T(8,128)S(1)}, f32[80,2048]{1,0:T(8,128)S(1)}, u32[]{:S(2)}, u32[]{:S(2)}) collective-permute-start(f32[80,2048]{1,0:T(8,128)S(1)} %collective-permute-done.8.refs_9_), channel_id=1, source_target_pairs={{0,4},{4,0},{8,12},{12,8},{16,20},{20,16},{24,28},{28,24},{1,5},{5... | collective-permute-start | bytes 1966088 | tf_op jit(solution)/shard_map/ppermute | solution.py:257
  180.4 17.7 %copy-start.13 = (f32[80,2048]{1,0:T(8,128)}, f32[80,2048]{1,0:T(8,128)S(1)}, u32[]{:S(2)}) copy-start(f32[80,2048]{1,0:T(8,128)S(1)} %collective-permute-done.1.refs_2_) | copy-start | bytes 1966084
  180.4 14.1 %collective-permute-start.5 = (f32[80,2048]{1,0:T(8,128)S(1)}, f32[80,2048]{1,0:T(8,128)S(1)}, u32[]{:S(2)}, u32[]{:S(2)}) collective-permute-start(f32[80,2048]{1,0:T(8,128)S(1)} %collective-permute-done.3.refs_4_), channel_id=1, source_target_pairs={{0,4},{4,0},{8,12},{12,8},{16,20},{20,16},{24,28},{28,24},{1,5},{5... | collective-permute-start | bytes 1966088 | tf_op jit(solution)/shard_map/ppermute | solution.py:257
  180.9 17.2 %copy-start.15 = (f32[80,2048]{1,0:T(8,128)}, f32[80,2048]{1,0:T(8,128)S(1)}, u32[]{:S(2)}) copy-start(f32[80,2048]{1,0:T(8,128)S(1)} %collective-permute-done.2.refs_3_) | copy-start | bytes 1966084
  180.9 13.6 %collective-permute-start.6 = (f32[80,2048]{1,0:T(8,128)S(1)}, f32[80,2048]{1,0:T(8,128)S(1)}, u32[]{:S(2)}, u32[]{:S(2)}) collective-permute-start(f32[80,2048]{1,0:T(8,128)S(1)} %collective-permute-done.4.refs_5_), channel_id=1, source_target_pairs={{0,4},{4,0},{8,12},{12,8},{16,20},{20,16},{24,28},{28,24},{1,5},{5... | collective-permute-start | bytes 1966088 | tf_op jit(solution)/shard_map/ppermute | solution.py:257
  193.2 4.9 %copy-start.17 = (f32[80,2048]{1,0:T(8,128)}, f32[80,2048]{1,0:T(8,128)S(1)}, u32[]{:S(2)}) copy-start(f32[80,2048]{1,0:T(8,128)S(1)} %collective-permute-done.11.refs_12_) | copy-start | bytes 1966084
  193.2 2.1 collective-permute-start.9
  194.0 4.1 %copy-start.19 = (f32[80,2048]{1,0:T(8,128)}, f32[80,2048]{1,0:T(8,128)S(1)}, u32[]{:S(2)}) copy-start(f32[80,2048]{1,0:T(8,128)S(1)} %collective-permute-done.12.refs_13_) | copy-start | bytes 1966084
  194.0 3.2 %collective-permute-start.13 = (f32[80,2048]{1,0:T(8,128)S(1)}, f32[80,2048]{1,0:T(8,128)S(1)}, u32[]{:S(2)}, u32[]{:S(2)}) collective-permute-start(f32[80,2048]{1,0:T(8,128)S(1)} %collective-permute-done.11.refs_12_), channel_id=1, source_target_pairs={{0,4},{4,0},{8,12},{12,8},{16,20},{20,16},{24,28},{28,24},{1,5},{5... | collective-permute-start | bytes 1966088 | tf_op jit(solution)/shard_map/ppermute | solution.py:257
  194.0 4.1 %copy-start.21 = (f32[80,2048]{1,0:T(8,128)}, f32[80,2048]{1,0:T(8,128)S(1)}, u32[]{:S(2)}) copy-start(f32[80,2048]{1,0:T(8,128)S(1)} %collective-permute-done.10.refs_11_) | copy-start | bytes 1966084
  194.0 4.0 %collective-permute-start.14 = (f32[80,2048]{1,0:T(8,128)S(1)}, f32[80,2048]{1,0:T(8,128)}, u32[]{:S(2)}, u32[]{:S(2)}) collective-permute-start(f32[80,2048]{1,0:T(8,128)S(1)} %collective-permute-done.12.refs_13_), channel_id=1, source_target_pairs={{0,4},{4,0},{8,12},{12,8},{16,20},{20,16},{24,28},{28,24},{1,5},{5... | collective-permute-start | bytes 1966088 | tf_op jit(solution)/shard_map/ppermute | solution.py:257
  194.5 3.6 %copy-start.23 = (f32[80,2048]{1,0:T(8,128)}, f32[80,2048]{1,0:T(8,128)S(1)}, u32[]{:S(2)}) copy-start(f32[80,2048]{1,0:T(8,128)S(1)} %collective-permute-done.5.refs_6_) | copy-start | bytes 1966084
  194.5 3.6 %copy-start.25 = (f32[80,2048]{1,0:T(8,128)}, f32[80,2048]{1,0:T(8,128)S(1)}, u32[]{:S(2)}) copy-start(f32[80,2048]{1,0:T(8,128)S(1)} %collective-permute-done.6.refs_7_) | copy-start | bytes 1966084
  195.3 2.8 copy-start.27
  197.2 0.9 copy-start.28
Sparse Core Ops, SparseCore 0:
  147.3 53.2 reduce-scatter.4
  248.8 52.4 reduce-scatter.2

commit v4 on v3

--- a/solution.py
+++ b/solution.py
@@ -246,6 +246,22 @@
     )(occ_irrep, vir_count, occ_energy, vir_energy, vir_t, *pieces)
 
 
+def after_kernel(array_ref, other_ref, out_ref):
+    pass
+
+
+def after(array, other):
+    anywhere = pl.BlockSpec(memory_space=pl.ANY)
+    return pl.pallas_call(
+        after_kernel,
+        out_shape=jax.ShapeDtypeStruct(array.shape, array.dtype),
+        in_specs=[anywhere, anywhere],
+        out_specs=anywhere,
+        input_output_aliases={0: 0},
+        cost_estimate=pl.CostEstimate(flops=0, bytes_accessed=0, transcendentals=0),
+    )(array, other)
+
+
 def on_device(t_cycle, w_cycle, occ_energy, vir_energy, occ_irrep, vir_count):
     n_pair = lax.axis_size("pair")
     n_ph = lax.axis_size("ph")
@@ -261,10 +277,12 @@
     own = compact_rows(occ_irrep, vir_count, parts, chunks)
     w_hi, w_lo = split_weights(occ_irrep, vir_count, w_cycle)
     pieces = []
+    earlier = w_hi
     for s in range(chunks):
         a, b = own[2 * s], own[2 * s + 1]
         near_a, near_b = swap(a, group), swap(b, group)
         far_a, far_b = swap(a, 2 * group), swap(b, 2 * group)
+        near_a, far_b = after(near_a, earlier), after(far_b, earlier)
         held = {0: (a, b), 1: (near_a, near_b), 2: (far_a, far_b)}
         held[3] = (swap(near_a, 2 * group), swap(far_b, group))
         rows = []
@@ -272,6 +290,7 @@
             for c in range(group):
                 rows += [array if c == 0 else swap(array, c) for array in held[q]]
         partial_value = product(occ_irrep, vir_count, s, rows, w_hi, w_lo, group)
+        earlier = partial_value
         summed = lax.psum_scatter(partial_value, "ph", scatter_dimension=0, tiled=True)
         if share > 1:
             groups = [[i * share + p for p in range(share)] for i in range(ROW_OCC)]

time: 313 us -> 303 us (0.968)
  waiting for transfers between devices: 140 us -> 132 us
    ppermute x29, waiting for transfers between devices: 88.4 us -> 79.6 us  [swap(): return lax.ppermute(array, 'pair', [(d, d ^ bits) for d in range(n_pair)])]
    unnamed x59 -> x53, local copies, waits for them, and re-layouts: 4.9 us -> 7.07 us
  transfers between devices with their start and end apart: 31 -> 31, of which waited for: 16 -> 13; matrix products, arithmetic and copies ran while one was open for 0% -> 0% of each run, Pallas kernels for 25% -> 25%
where the time goes in v4:
time: 303 us; the launch traced here: 302 us
  Pallas kernels  134 us (44%)
  waiting for transfers between devices  132 us (44%)
  starting transfers between devices  15.5 us (5%)
  between operations  13.6 us (4%)
  local copies, waits for them, and re-layouts  7.07 us (2%)
    pallas_call x2, Pallas kernels, product(): pl.pallas_call(functools.partial(product_kernel, group, chunk), out_shape...  88.5 us
    ppermute x29, waiting for transfers between devices, swap(): return lax.ppermute(array, 'pair', [(d, d ^ bits) for d in range(n_pair)])  79.6 us
    reduce_scatter x2, waiting for transfers between devices, on_device(): lax.psum_scatter(partial_value, 'ph', scatter_dimension=0, tiled=True)  52 us
    pallas_call x1, Pallas kernels, split_weights(): pl.pallas_call(split_kernel, out_shape=(part, part), grid_spec=pltpu.Pref...  29.4 us
    ppermute x29, starting transfers between devices, swap(): return lax.ppermute(array, 'pair', [(d, d ^ bits) for d in range(n_pair)])  15.5 us
    pallas_call x1, Pallas kernels, compact_rows(): pl.pallas_call(functools.partial(compact_kernel, group), out_shape=[jax.S...  10.9 us
    unnamed x53, local copies, waits for them, and re-layouts  7.07 us
  transfers between devices with their start and end apart: 31, of which 13 were waited for; matrix products, arithmetic and copies ran while one was open for 0% of the time, Pallas kernels for 25%

profile of v4, /device:TPU:0, one launch (start us, length us, event | category | flops | bytes accessed | tf_op | source)
XLA Modules:
  0.0 301.8 jit_solution(711421201324689222)
XLA Ops:
  6.5 0.5 collective-permute-start
  7.0 7.0 %collective-permute-done.refs_1_ = f32[8,64,2048]{2,1,0:T(8,128)S(1)} collective-permute-done((f32[8,64,2048]{2,1,0:T(8,128)}, f32[8,64,2048]{2,1,0:T(8,128)S(1)}, u32[]{:S(2)}, u32[]{:S(2)}) %collective-permute-start) | collective-permute-done | bytes 4194336 | tf_op jit(solution)/shard_map/ppermute | solution.py:273
  14.0 2.0 copy-done
  16.0 10.9 %shard_map.64 = (f32[80,2048]{1,0:T(8,128)}, f32[80,2048]{1,0:T(8,128)}, f32[80,2048]{1,0:T(8,128)}, f32[80,2048]{1,0:T(8,128)}) custom-call(s32[64]{0:T(128)} %irrep_ref.9, s32[8]{0:T(128)} %count_ref.9, f32[8,64,2048]{2,1,0:T(8,128)} %refs_0_.1, f32[8,64,2048]{2,1,0:T(8,128)} %copy-done), custom_call_target="tpu_custom_call" | custom-call | tf_op jit(solution)/shard_map/pallas_call | solution.py:103
  26.9 2.9 collective-permute-start.3
  29.7 1.5 collective-permute-start.8
  31.3 0.0 collective-permute-start.1
  31.3 0.5 collective-permute-start.2
  31.8 29.4 %shard_map.65 = (bf16[8,2048,512]{2,1,0:T(8,128)(2,1)}, bf16[8,2048,512]{2,1,0:T(8,128)(2,1)}) custom-call(s32[64]{0:T(128)} %irrep_ref.9, s32[8]{0:T(128)} %count_ref.9, f32[8,2048,512]{2,1,0:T(8,128)} %w_ref.1), custom_call_target="tpu_custom_call" | custom-call | flops 33554432 | bytes 67108864 | tf_op jit(solution)/shard_map/pallas_call | solution.py:52
  61.1 0.5 collective-permute-start.4
  61.7 0.1 collective-permute-start.7
  61.8 0.8 copy-done.2
  62.5 0.1 collective-permute-start.5
  62.6 0.8 copy-done.1
  63.4 0.0 collective-permute-done.1.refs_2_
  63.4 0.5 copy-done.3
  63.9 1.2 collective-permute-start.11
  65.1 0.0 collective-permute-done.2.refs_3_
  65.1 1.5 collective-permute-start.12
  66.6 12.2 %collective-permute-done.4.refs_5_ = f32[80,2048]{1,0:T(8,128)} collective-permute-done((f32[80,2048]{1,0:T(8,128)S(1)}, f32[80,2048]{1,0:T(8,128)}, u32[]{:S(2)}, u32[]{:S(2)}) %collective-permute-start.4) | collective-permute-done | bytes 655392 | tf_op jit(solution)/shard_map/ppermute | solution.py:273
  78.8 0.0 collective-permute-start.10
  78.8 0.6 collective-permute-done.7.refs_8_
  79.5 0.0 collective-permute-start.6
  79.5 0.0 collective-permute-done.5.refs_6_
  79.5 0.5 collective-permute-start.9
  80.0 12.1 %collective-permute-done.11.refs_12_ = f32[80,2048]{1,0:T(8,128)S(1)} collective-permute-done((f32[80,2048]{1,0:T(8,128)S(1)}, f32[80,2048]{1,0:T(8,128)S(1)}, u32[]{:S(2)}, u32[]{:S(2)}) %collective-permute-start.11) | collective-permute-done | bytes 655392 | tf_op jit(solution)/shard_map/ppermute | solution.py:273
  92.1 0.0 collective-permute-start.13
  92.1 0.0 collective-permute-done.12.refs_13_
  92.2 0.5 collective-permute-start.14
  92.7 0.0 collective-permute-done.6.refs_7_
  92.7 0.0 collective-permute-done.10.refs_11_
  92.7 1.5 collective-permute-done.13.refs_14_
  94.2 0.9 collective-permute-done.14.refs_15_
  95.2 0.8 copy-done.25
  96.0 41.3 %shard_map.68 = f32[4,320,512]{2,1,0:T(8,128)} custom-call(s32[64]{0:T(128)} %irrep_ref.9, s32[8]{0:T(128)} %count_ref.9, f32[80,2048]{1,0:T(8,128)} %get-tuple-element.11.refs_0_, f32[80,2048]{1,0:T(8,128)} %get-tuple-element.12.refs_1_, f32[80,2048]{1,0:T(8,128)} %copy-done.12, f32[80,2048]{1,0:T(8,128)} %collective-permute-done.2.refs_3_, ...), custom_call_target="tpu_custom_call" | custom-call | flops 32212254720 | bytes 41943040 | tf_op jit(solution)/shard_map/pallas_call | solution.py:172
  137.4 0.0 reduce-scatter.3.cloned.1.call-update
  137.4 0.0 reduce-scatter.5.cloned.1.call-start
  137.4 1.6 collective-permute-start.17
  139.0 0.5 collective-permute-start.18
  139.5 0.3 collective-permute-start.22
  139.8 0.5 collective-permute-start.16
  140.3 14.8 %collective-permute-done.17.array_ref = f32[80,2048]{1,0:T(8,128)S(1)} collective-permute-done((f32[80,2048]{1,0:T(8,128)S(1)}, f32[80,2048]{1,0:T(8,128)S(1)}, u32[]{:S(2)}, u32[]{:S(2)}) %collective-permute-start.17) | collective-permute-done | bytes 655392 | tf_op jit(solution)/shard_map/ppermute | solution.py:273
  155.1 0.3 collective-permute-start.21
  155.4 13.0 %collective-permute-done.18.refs_5_ = f32[80,2048]{1,0:T(8,128)S(1)} collective-permute-done((f32[80,2048]{1,0:T(8,128)S(1)}, f32[80,2048]{1,0:T(8,128)S(1)}, u32[]{:S(2)}, u32[]{:S(2)}) %collective-permute-start.18) | collective-permute-done | bytes 655392 | tf_op jit(solution)/shard_map/ppermute | solution.py:273
  168.4 0.3 collective-permute-start.25
  168.7 0.6 copy-done.5
  169.3 1.5 collective-permute-start.26
  170.8 0.0 collective-permute-done.21.refs_8_
  170.8 0.2 collective-permute-start.23
  170.9 0.3 collective-permute-start.19
  171.3 0.2 collective-permute-start.24
  171.5 14.4 %collective-permute-done.25.refs_12_ = f32[80,2048]{1,0:T(8,128)} collective-permute-done((f32[80,2048]{1,0:T(8,128)}, f32[80,2048]{1,0:T(8,128)}, u32[]{:S(2)}, u32[]{:S(2)}) %collective-permute-start.25) | collective-permute-done | bytes 655392 | tf_op jit(solution)/shard_map/ppermute | solution.py:273
  185.9 0.7 collective-permute-done.26.refs_13_
  186.6 0.0 collective-permute-done.19.refs_6_
  186.6 0.0 collective-permute-done.24.refs_11_
  186.6 1.5 collective-permute-done.27.refs_14_
  188.2 0.7 collective-permute-done.28.refs_15_
  188.9 0.1 copy-done.22
  189.0 0.8 copy-done.24
  189.9 47.1 %shard_map.71 = f32[4,320,512]{2,1,0:T(8,128)} custom-call(s32[64]{0:T(128)} %irrep_ref.9, s32[8]{0:T(128)} %count_ref.9, f32[80,2048]{1,0:T(8,128)} %get-tuple-element.15.refs_0_, f32[80,2048]{1,0:T(8,128)} %get-tuple-element.16.refs_1_, f32[80,2048]{1,0:T(8,128)} %collective-permute-done.15.refs_2_, f32[80,2048]{1,0:T(8,128)} %collective-permute-done.16.refs_3_, ...), custom_call_target="tpu_custom_call" | custom-call | flops 32212254720 | bytes 41943040 | tf_op jit(solution)/shard_map/pallas_call | solution.py:172
  237.0 0.0 reduce-scatter.5.cloned.1.call-update
  237.1 0.7 copy.11
  237.8 52.0 %reduce-scatter.5.cloned.1.call-done.refs_1_ = f32[320,512]{1,0:T(8,128)} async-done(((f32[1280,512]{1,0:T(8,128)}), f32[320,512]{1,0:T(8,128)}) %reduce-scatter.5.cloned.1.call-update) | async-done | bytes 655376 | tf_op jit(solution)/shard_map/reduce_scatter | solution.py:294
  289.8 5.2 %shard_map.72 = f32[8,128,512]{2,1,0:T(8,128)} custom-call(s32[64]{0:T(128)} %irrep_ref.9, s32[8]{0:T(128)} %count_ref.9, f32[64]{0:T(128)} %occ_ref.1, f32[8,128]{1,0:T(8,128)} %vir_ref.1, f32[128,8]{1,0:T(8,128)} %bitcast.7, f32[320,512]{1,0:T(8,128)} %reduce-scatter.3.cloned.1.call-done.refs_0_, f32[320,512]{1,0:T(8,128)} %reduce-scatter.5.cloned.1.call-done.refs_1_), custom_call_target="tpu_custom_call" | custom-call | tf_op jit(solution)/shard_map/pallas_call | solution.py:238
  (62 shorter events, 0.1 us)
Async XLA Ops:
  6.5 231.2 %reduce-scatter.3.cloned.1.call-start = ((), (), s32[]{:S(2)}) async-start(), calls=%async_computation.2 | async-start | bytes 3276800 | tf_op jit(solution)/shard_map/reduce_scatter | solution.py:294
  6.5 7.4 %collective-permute-start = (f32[8,64,2048]{2,1,0:T(8,128)}, f32[8,64,2048]{2,1,0:T(8,128)S(1)}, u32[]{:S(2)}, u32[]{:S(2)}) collective-permute-start(f32[8,64,2048]{2,1,0:T(8,128)} %refs_0_.1), channel_id=1, source_target_pairs={{0,4},{4,0},{8,12},{12,8},{16,20},{20,16},{24,28},{28,24},{1,5},{5... | collective-permute-start | bytes 12582920 | tf_op jit(solution)/shard_map/ppermute | solution.py:273
  14.0 2.0 copy-start
  26.9 34.8 %collective-permute-start.3 = (f32[80,2048]{1,0:T(8,128)}, f32[80,2048]{1,0:T(8,128)S(1)}, u32[]{:S(2)}, u32[]{:S(2)}) collective-permute-start(f32[80,2048]{1,0:T(8,128)} %get-tuple-element.11.refs_0_), channel_id=1, source_target_pairs={{0,8},{4,12},{8,0},{12,4},{16,24},{20,28},{24,16},{28,20},{1,9},{5... | collective-permute-start | bytes 1966088 | tf_op jit(solution)/shard_map/ppermute | solution.py:273
  29.7 31.4 %copy-start.10 = (f32[80,2048]{1,0:T(8,128)S(1)}, f32[80,2048]{1,0:T(8,128)}, u32[]{:S(2)}) copy-start(f32[80,2048]{1,0:T(8,128)} %get-tuple-element.12.refs_1_) | copy-start | bytes 1966084
  29.7 31.9 %copy-start.9 = (f32[80,2048]{1,0:T(8,128)S(1)}, f32[80,2048]{1,0:T(8,128)}, u32[]{:S(2)}) copy-start(f32[80,2048]{1,0:T(8,128)} %get-tuple-element.11.refs_0_) | copy-start | bytes 1966084
  29.7 32.8 %collective-permute-start.8 = (f32[80,2048]{1,0:T(8,128)}, f32[80,2048]{1,0:T(8,128)S(1)}, u32[]{:S(2)}, u32[]{:S(2)}) collective-permute-start(f32[80,2048]{1,0:T(8,128)} %get-tuple-element.12.refs_1_), channel_id=1, source_target_pairs={{0,16},{4,20},{8,24},{12,28},{16,0},{20,4},{24,8},{28,12},{1,17},{... | collective-permute-start | bytes 1966088 | tf_op jit(solution)/shard_map/ppermute | solution.py:273
  31.3 32.1 %collective-permute-start.1 = (f32[80,2048]{1,0:T(8,128)}, f32[80,2048]{1,0:T(8,128)S(1)}, u32[]{:S(2)}, u32[]{:S(2)}) collective-permute-start(f32[80,2048]{1,0:T(8,128)} %get-tuple-element.11.refs_0_), channel_id=1, source_target_pairs={{0,4},{4,0},{8,12},{12,8},{16,20},{20,16},{24,28},{28,24},{1,5},{5... | collective-permute-start | bytes 1966088 | tf_op jit(solution)/shard_map/ppermute | solution.py:273
  31.3 33.8 %collective-permute-start.2 = (f32[80,2048]{1,0:T(8,128)}, f32[80,2048]{1,0:T(8,128)}, u32[]{:S(2)}, u32[]{:S(2)}) collective-permute-start(f32[80,2048]{1,0:T(8,128)} %get-tuple-element.12.refs_1_), channel_id=1, source_target_pairs={{0,4},{4,0},{8,12},{12,8},{16,20},{20,16},{24,28},{28,24},{1,5},{5... | collective-permute-start | bytes 1966088 | tf_op jit(solution)/shard_map/ppermute | solution.py:273
  61.1 17.7 %collective-permute-start.4 = (f32[80,2048]{1,0:T(8,128)S(1)}, f32[80,2048]{1,0:T(8,128)}, u32[]{:S(2)}, u32[]{:S(2)}) collective-permute-start(f32[80,2048]{1,0:T(8,128)S(1)} %copy-done.10), channel_id=1, source_target_pairs={{0,8},{4,12},{8,0},{12,4},{16,24},{20,28},{24,16},{28,20},{1,9},{5... | collective-permute-start | bytes 1966088 | tf_op jit(solution)/shard_map/ppermute | solution.py:273
  61.7 0.9 copy-start.2
  61.7 17.8 %collective-permute-start.7 = (f32[80,2048]{1,0:T(8,128)S(1)}, f32[80,2048]{1,0:T(8,128)}, u32[]{:S(2)}, u32[]{:S(2)}) collective-permute-start(f32[80,2048]{1,0:T(8,128)S(1)} %copy-done.9), channel_id=1, source_target_pairs={{0,16},{4,20},{8,24},{12,28},{16,0},{20,4},{24,8},{28,12},{1,17},{... | collective-permute-start | bytes 1966088 | tf_op jit(solution)/shard_map/ppermute | solution.py:273
  62.5 1.3 copy-start.3
  62.5 0.9 copy-start.1
  62.5 16.9 %collective-permute-start.5 = (f32[80,2048]{1,0:T(8,128)}, f32[80,2048]{1,0:T(8,128)}, u32[]{:S(2)}, u32[]{:S(2)}) collective-permute-start(f32[80,2048]{1,0:T(8,128)} %shard_map.66.refs_4_), channel_id=1, source_target_pairs={{0,4},{4,0},{8,12},{12,8},{16,20},{20,16},{24,28},{28,24},{1,5},{5... | collective-permute-start | bytes 1966088 | tf_op jit(solution)/shard_map/ppermute | solution.py:273
  63.9 31.3 %copy-start.12 = (f32[80,2048]{1,0:T(8,128)}, f32[80,2048]{1,0:T(8,128)S(1)}, u32[]{:S(2)}) copy-start(f32[80,2048]{1,0:T(8,128)S(1)} %collective-permute-done.1.refs_2_) | copy-start | bytes 1966084
  63.9 28.3 %collective-permute-start.11 = (f32[80,2048]{1,0:T(8,128)S(1)}, f32[80,2048]{1,0:T(8,128)S(1)}, u32[]{:S(2)}, u32[]{:S(2)}) collective-permute-start(f32[80,2048]{1,0:T(8,128)S(1)} %copy-done.3), channel_id=1, source_target_pairs={{0,16},{4,20},{8,24},{12,28},{16,0},{20,4},{24,8},{28,12},{1,17},{... | collective-permute-start | bytes 1966088 | tf_op jit(solution)/shard_map/ppermute | solution.py:273
  65.1 27.1 %collective-permute-start.12 = (f32[80,2048]{1,0:T(8,128)}, f32[80,2048]{1,0:T(8,128)S(1)}, u32[]{:S(2)}, u32[]{:S(2)}) collective-permute-start(f32[80,2048]{1,0:T(8,128)} %shard_map.67.refs_9_), channel_id=1, source_target_pairs={{0,8},{4,12},{8,0},{12,4},{16,24},{20,28},{24,16},{28,20},{1,9},{5... | collective-permute-start | bytes 1966088 | tf_op jit(solution)/shard_map/ppermute | solution.py:273
  78.8 13.8 %collective-permute-start.10 = (f32[80,2048]{1,0:T(8,128)}, f32[80,2048]{1,0:T(8,128)S(1)}, u32[]{:S(2)}, u32[]{:S(2)}) collective-permute-start(f32[80,2048]{1,0:T(8,128)} %shard_map.67.refs_9_), channel_id=1, source_target_pairs={{0,4},{4,0},{8,12},{12,8},{16,20},{20,16},{24,28},{28,24},{1,5},{5... | collective-permute-start | bytes 1966088 | tf_op jit(solution)/shard_map/ppermute | solution.py:273
  79.5 13.2 %collective-permute-start.6 = (f32[80,2048]{1,0:T(8,128)}, f32[80,2048]{1,0:T(8,128)S(1)}, u32[]{:S(2)}, u32[]{:S(2)}) collective-permute-start(f32[80,2048]{1,0:T(8,128)} %collective-permute-done.4.refs_5_), channel_id=1, source_target_pairs={{0,4},{4,0},{8,12},{12,8},{16,20},{20,16},{24,28},{28,24},{1,5},{5... | collective-permute-start | bytes 1966088 | tf_op jit(solution)/shard_map/ppermute | solution.py:273
  79.5 13.2 %collective-permute-start.9 = (f32[80,2048]{1,0:T(8,128)}, f32[80,2048]{1,0:T(8,128)S(1)}, u32[]{:S(2)}, u32[]{:S(2)}) collective-permute-start(f32[80,2048]{1,0:T(8,128)} %collective-permute-done.7.refs_8_), channel_id=1, source_target_pairs={{0,4},{4,0},{8,12},{12,8},{16,20},{20,16},{24,28},{28,24},{1,5},{5... | collective-permute-start | bytes 1966088 | tf_op jit(solution)/shard_map/ppermute | solution.py:273
  92.1 3.0 %copy-start.13 = (f32[80,2048]{1,0:T(8,128)}, f32[80,2048]{1,0:T(8,128)S(1)}, u32[]{:S(2)}) copy-start(f32[80,2048]{1,0:T(8,128)S(1)} %collective-permute-done.11.refs_12_) | copy-start | bytes 1966084
  92.1 2.1 collective-permute-start.13
  92.2 3.0 %copy-start.15 = (f32[80,2048]{1,0:T(8,128)}, f32[80,2048]{1,0:T(8,128)S(1)}, u32[]{:S(2)}) copy-start(f32[80,2048]{1,0:T(8,128)S(1)} %collective-permute-done.12.refs_13_) | copy-start | bytes 1966084
  92.2 3.0 collective-permute-start.14
  92.7 2.5 copy-start.19
  92.7 2.5 copy-start.21
  92.7 2.5 copy-start.17
  94.2 1.0 copy-start.23
  95.2 0.8 copy-start.25
  96.0 41.4 %copy-start.7 = (f32[80,2048]{1,0:T(8,128)S(1)}, f32[80,2048]{1,0:T(8,128)}, u32[]{:S(2)}) copy-start(f32[80,2048]{1,0:T(8,128)} %get-tuple-element.15.refs_0_) | copy-start | bytes 1966084
  96.0 43.0 %copy-start.8 = (f32[80,2048]{1,0:T(8,128)S(1)}, f32[80,2048]{1,0:T(8,128)}, u32[]{:S(2)}) copy-start(f32[80,2048]{1,0:T(8,128)} %get-tuple-element.16.refs_1_) | copy-start | bytes 1966084
  137.4 152.4 %reduce-scatter.5.cloned.1.call-start = ((), (), s32[]{:S(2)}) async-start(), calls=%async_computation.3 | async-start | bytes 3276800 | tf_op jit(solution)/shard_map/reduce_scatter | solution.py:294
  137.4 17.6 %collective-permute-start.17 = (f32[80,2048]{1,0:T(8,128)S(1)}, f32[80,2048]{1,0:T(8,128)S(1)}, u32[]{:S(2)}, u32[]{:S(2)}) collective-permute-start(f32[80,2048]{1,0:T(8,128)S(1)} %copy-done.7), channel_id=1, source_target_pairs={{0,8},{4,12},{8,0},{12,4},{16,24},{20,28},{24,16},{28,20},{1,9},{5... | collective-permute-start | bytes 1966088 | tf_op jit(solution)/shard_map/ppermute | solution.py:273
  139.0 29.3 %collective-permute-start.18 = (f32[80,2048]{1,0:T(8,128)S(1)}, f32[80,2048]{1,0:T(8,128)S(1)}, u32[]{:S(2)}, u32[]{:S(2)}) collective-permute-start(f32[80,2048]{1,0:T(8,128)S(1)} %copy-done.8), channel_id=1, source_target_pairs={{0,8},{4,12},{8,0},{12,4},{16,24},{20,28},{24,16},{28,20},{1,9},{5... | collective-permute-start | bytes 1966088 | tf_op jit(solution)/shard_map/ppermute | solution.py:273
  139.5 28.8 %collective-permute-start.22 = (f32[80,2048]{1,0:T(8,128)S(1)}, f32[80,2048]{1,0:T(8,128)S(1)}, u32[]{:S(2)}, u32[]{:S(2)}) collective-permute-start(f32[80,2048]{1,0:T(8,128)S(1)} %copy-done.8), channel_id=1, source_target_pairs={{0,16},{4,20},{8,24},{12,28},{16,0},{20,4},{24,8},{28,12},{1,17},{... | collective-permute-start | bytes 1966088 | tf_op jit(solution)/shard_map/ppermute | solution.py:273
  139.8 29.5 %collective-permute-start.15 = (f32[80,2048]{1,0:T(8,128)S(1)}, f32[80,2048]{1,0:T(8,128)}, u32[]{:S(2)}, u32[]{:S(2)}) collective-permute-start(f32[80,2048]{1,0:T(8,128)S(1)} %copy-done.7), channel_id=1, source_target_pairs={{0,4},{4,0},{8,12},{12,8},{16,20},{20,16},{24,28},{28,24},{1,5},{5... | collective-permute-start | bytes 1966088 | tf_op jit(solution)/shard_map/ppermute | solution.py:273
  139.8 31.1 %collective-permute-start.16 = (f32[80,2048]{1,0:T(8,128)S(1)}, f32[80,2048]{1,0:T(8,128)}, u32[]{:S(2)}, u32[]{:S(2)}) collective-permute-start(f32[80,2048]{1,0:T(8,128)S(1)} %copy-done.8), channel_id=1, source_target_pairs={{0,4},{4,0},{8,12},{12,8},{16,20},{20,16},{24,28},{28,24},{1,5},{5... | collective-permute-start | bytes 1966088 | tf_op jit(solution)/shard_map/ppermute | solution.py:273
  155.1 13.3 %copy-start.4 = (f32[80,2048]{1,0:T(8,128)}, f32[80,2048]{1,0:T(8,128)S(1)}, u32[]{:S(2)}) copy-start(f32[80,2048]{1,0:T(8,128)S(1)} %collective-permute-done.17.array_ref) | copy-start | bytes 1966084
  155.1 15.7 %collective-permute-start.21 = (f32[80,2048]{1,0:T(8,128)S(1)}, f32[80,2048]{1,0:T(8,128)}, u32[]{:S(2)}, u32[]{:S(2)}) collective-permute-start(f32[80,2048]{1,0:T(8,128)S(1)} %copy-done.7), channel_id=1, source_target_pairs={{0,16},{4,20},{8,24},{12,28},{16,0},{20,4},{24,8},{28,12},{1,17},{... | collective-permute-start | bytes 1966088 | tf_op jit(solution)/shard_map/ppermute | solution.py:273
  168.3 20.6 %copy-start.11 = (f32[80,2048]{1,0:T(8,128)}, f32[80,2048]{1,0:T(8,128)S(1)}, u32[]{:S(2)}) copy-start(f32[80,2048]{1,0:T(8,128)S(1)} %collective-permute-done.18.refs_5_) | copy-start | bytes 1966084
  168.3 3.0 collective-permute-start.20
  168.4 0.9 copy-start.5
  168.4 17.5 %collective-permute-start.25 = (f32[80,2048]{1,0:T(8,128)}, f32[80,2048]{1,0:T(8,128)}, u32[]{:S(2)}, u32[]{:S(2)}) collective-permute-start(f32[80,2048]{1,0:T(8,128)} %shard_map.69.refs_4_), channel_id=1, source_target_pairs={{0,16},{4,20},{8,24},{12,28},{16,0},{20,4},{24,8},{28,12},{1,17},{... | collective-permute-start | bytes 1966088 | tf_op jit(solution)/shard_map/ppermute | solution.py:273
  169.3 67.8 %copy-start.6 = (f32[8,128]{1,0:T(8,128)S(1)}, f32[8,128]{1,0:T(8,128)}, u32[]{:S(2)}) copy-start(f32[8,128]{1,0:T(8,128)} %vir_ref.1) | copy-start | bytes 12292
  169.3 17.3 %collective-permute-start.26 = (f32[80,2048]{1,0:T(8,128)}, f32[80,2048]{1,0:T(8,128)S(1)}, u32[]{:S(2)}, u32[]{:S(2)}) collective-permute-start(f32[80,2048]{1,0:T(8,128)} %shard_map.70.refs_9_), channel_id=1, source_target_pairs={{0,8},{4,12},{8,0},{12,4},{16,24},{20,28},{24,16},{28,20},{1,9},{5... | collective-permute-start | bytes 1966088 | tf_op jit(solution)/shard_map/ppermute | solution.py:273
  170.8 15.8 %collective-permute-start.23 = (f32[80,2048]{1,0:T(8,128)}, f32[80,2048]{1,0:T(8,128)S(1)}, u32[]{:S(2)}, u32[]{:S(2)}) collective-permute-start(f32[80,2048]{1,0:T(8,128)} %collective-permute-done.21.refs_8_), channel_id=1, source_target_pairs={{0,4},{4,0},{8,12},{12,8},{16,20},{20,16},{24,28},{28,24},{1,5},{5... | collective-permute-start | bytes 1966088 | tf_op jit(solution)/shard_map/ppermute | solution.py:273
  170.9 15.7 %collective-permute-start.19 = (f32[80,2048]{1,0:T(8,128)}, f32[80,2048]{1,0:T(8,128)S(1)}, u32[]{:S(2)}, u32[]{:S(2)}) collective-permute-start(f32[80,2048]{1,0:T(8,128)} %shard_map.69.refs_4_), channel_id=1, source_target_pairs={{0,4},{4,0},{8,12},{12,8},{16,20},{20,16},{24,28},{28,24},{1,5},{5... | collective-permute-start | bytes 1966088 | tf_op jit(solution)/shard_map/ppermute | solution.py:273
  171.3 15.3 %collective-permute-start.24 = (f32[80,2048]{1,0:T(8,128)}, f32[80,2048]{1,0:T(8,128)S(1)}, u32[]{:S(2)}, u32[]{:S(2)}) collective-permute-start(f32[80,2048]{1,0:T(8,128)} %shard_map.70.refs_9_), channel_id=1, source_target_pairs={{0,4},{4,0},{8,12},{12,8},{16,20},{20,16},{24,28},{28,24},{1,5},{5... | collective-permute-start | bytes 1966088 | tf_op jit(solution)/shard_map/ppermute | solution.py:273
  185.9 2.3 collective-permute-start.27
  186.6 2.3 copy-start.14
  186.6 2.3 collective-permute-start.28
  186.6 2.3 copy-start.16
  186.6 2.3 copy-start.18
  186.6 2.3 copy-start.20
  188.2 0.9 copy-start.22
  189.0 0.8 copy-start.24
Sparse Core Ops, SparseCore 0:
  137.5 52.4 reduce-scatter.2
  237.2 52.5 reduce-scatter.4
